TPU v7x, 32 devices: a whole 2x2x4 slice. The times are simulated.
32 devices in a mesh: blk: 8 (over y, x, core), dp: 4 (over z).
Axes of the slice: x: 2, y: 2, z: 4, core: 2. Of those that a mesh axis runs over, the one named last changes fastest.
Arguments:
- inputs: bfloat16 [8, 1024, 768], P('dp', 'blk'), may hold values from -6 to 6
- lengths: int32 [8], P('dp'), may hold values from 64 to 1024, as said below
- prenorm: bfloat16 [768], P(('blk', 'dp')), may hold values from 0.099609375 to 1.8984375
- midnorm: bfloat16 [768], P(('blk', 'dp')), may hold values from 0.099609375 to 1.8984375
- query_proj: bfloat16 [768, 768], P(('blk', 'dp')), may hold values from -0.21875 to 0.21875
- key_proj: bfloat16 [768, 768], P(('blk', 'dp')), may hold values from -0.21875 to 0.21875
- value_proj: bfloat16 [768, 768], P(('blk', 'dp')), may hold values from -0.21875 to 0.21875
- output_proj: bfloat16 [768, 768], P(('blk', 'dp')), may hold values from -0.875 to 0.875
- premix: float32 [12, 12], replicated, may hold values from -1.75 to 1.75
- postmix: float32 [12, 12], replicated, may hold values from -1.75 to 1.75
- inner_proj: bfloat16 [768, 3072], P(('blk', 'dp')), may hold values from -0.21875 to 0.21875
- outer_proj: bfloat16 [3072, 768], P(('blk', 'dp')), may hold values from -0.109375 to 0.109375
- cotangent: bfloat16 [8, 1024, 768], P('dp', 'blk'), may hold values from -6 to 6
Outputs:
- outputs: bfloat16 [8, 1024, 768], P('dp', 'blk')
- grad_inputs: bfloat16 [8, 1024, 768], P('dp', 'blk')
- grad_prenorm: float32 [768], P(('blk', 'dp'))
- grad_midnorm: float32 [768], P(('blk', 'dp'))
- grad_query: float32 [768, 768], P(('blk', 'dp'))
- grad_key: float32 [768, 768], P(('blk', 'dp'))
- grad_value: float32 [768, 768], P(('blk', 'dp'))
- grad_output: float32 [768, 768], P(('blk', 'dp'))
- grad_premix: float32 [12, 12], replicated
- grad_postmix: float32 [12, 12], replicated
- grad_inner: float32 [768, 3072], P(('blk', 'dp'))
- grad_outer: float32 [3072, 768], P(('blk', 'dp'))
Inputs may be any that keep to these rules, and one draw needn't show every extreme that they name: `lengths`: in each aligned group of 2 rows (the rows of one index of dp) one row, chosen by the seed, has length 1024; positions at or past a row's length are padding.
All inputs are finite; a program needn't handle non-finite values.
Results may differ from a plain program's by a relative error of at most 0.017.
Values may be sent and summed in bfloat16 or wider, within the bound.
No kernel may reach another device: no remote copies, remote signals or barrier semaphores. Data moves between devices by JAX's collectives and lax.ppermute only.
A program may use at most 128 MiB of HBM per device.

v0:
```python
import jax
import jax.numpy as jnp
from jax import lax
from jax.sharding import PartitionSpec as P

NEGATIVE = -1e30
EPSILON = 1e-06
HIGH = lax.Precision.HIGHEST


def as_sent(shard):

    def short(part):
        return part.astype(jnp.bfloat16) if part.dtype == jnp.float32 else part

    return jax.tree.map(short, shard)


def shifted(value, axis, steps):
    count = lax.axis_size(axis)
    first, last = (max(0, -steps), min(count, count - steps))
    return lax.ppermute(value, axis, [(source, source + steps) for source in range(first, last)])


def from_behind(block, axis, distance):
    devices = range(lax.axis_size(axis))
    route = [((i - distance) % len(devices), i) for i in devices]
    return lax.ppermute(block, axis, route)


def normalize(values, gain):
    return values * lax.rsqrt(jnp.mean(values * values, axis=-1, keepdims=True) + EPSILON) * gain


def smooth(values):
    return jax.nn.gelu(values, approximate=True)


def block_mask(lengths, query_block, key_block, width):
    offsets = jnp.arange(width, dtype=jnp.int32)
    query_pos = query_block * width + offsets
    key_pos = key_block * width + offsets
    causal = key_pos[None, :] <= query_pos[:, None]
    inside = key_pos[None, :] < lengths[:, None]
    return causal[None, None] & inside[:, None, None, :]


def block_logits(queries, keys, premix, allowed):
    scores = (
        jnp.einsum("rihd,rjhd->rhij", queries, keys, preferred_element_type=jnp.float32) * 0.125
    )
    logits = jnp.einsum("gh,rgij->rhij", premix, scores, precision=HIGH)
    return (scores, jnp.where(allowed, logits, NEGATIVE))


def pair_grads(queries, upstream, log_total, dot_sum, keys, values, allowed, premix, postmix):
    scores, logits = block_logits(queries, keys, premix, allowed)
    softmax_out = jnp.where(allowed, jnp.exp(logits - log_total[..., None]), 0.0)
    mixed = jnp.einsum("hk,rhij->rkij", postmix, softmax_out, precision=HIGH).astype(jnp.bfloat16)
    mixed_grad = jnp.einsum("rikd,rjkd->rkij", upstream, values, preferred_element_type=jnp.float32)
    prob_grad = jnp.einsum("hk,rkij->rhij", postmix, mixed_grad, precision=HIGH)
    logit_grad = softmax_out * (prob_grad - dot_sum[..., None])
    score_grad = jnp.einsum("gh,rhij->rgij", premix, logit_grad, precision=HIGH).astype(
        jnp.bfloat16
    )
    query_term = (
        jnp.einsum("rgij,rjgd->rigd", score_grad, keys, preferred_element_type=jnp.float32) * 0.125
    )
    key_term = (
        jnp.einsum("rgij,rigd->rjgd", score_grad, queries, preferred_element_type=jnp.float32)
        * 0.125
    )
    value_term = jnp.einsum("rkij,rikd->rjkd", mixed, upstream, preferred_element_type=jnp.float32)
    pre_term = jnp.einsum("rgij,rhij->gh", scores, logit_grad, precision=HIGH)
    post_term = jnp.einsum("rhij,rkij->hk", softmax_out, mixed_grad, precision=HIGH)
    return (query_term, key_term, value_term, pre_term, post_term)


def key_cycle(pair, visit, carry):
    place = lax.axis_index("blk")
    count = lax.axis_size("blk")

    def one_turn(turn, state):
        key_block = place - turn
        return lax.cond(
            key_block >= 0,
            lambda inner: visit(inner, state[1], key_block),
            lambda inner: inner,
            state[0],
        )

    def key_advance(turn, state):
        carried = one_turn(turn, state)
        moved = shifted(as_sent(state[1]), "blk", 1)
        return (carried, moved)

    state = lax.fori_loop(0, count - 1, key_advance, (carry, pair))
    return one_turn(count - 1, state)


def keys_circle(queries, upstream, log_total, dot_sum, keys, values, lengths, premix, postmix):
    place = lax.axis_index("blk")
    count = lax.axis_size("blk")
    width = queries.shape[1]

    def visit(turn, state):
        local, pair, sums = state
        key_block = (place - turn) % count

        def work(inner):
            local_in, sums_in = inner
            allowed = block_mask(lengths, place, key_block, width)
            terms = pair_grads(
                queries, upstream, log_total, dot_sum, pair[0], pair[1], allowed, premix, postmix
            )
            return (
                (local_in[0] + terms[0], local_in[1] + terms[3], local_in[2] + terms[4]),
                (sums_in[0] + terms[1], sums_in[1] + terms[2]),
            )

        return lax.cond(key_block <= place, work, lambda inner: inner, (local, sums))

    def keys_advance(turn, state):
        local, sums = visit(turn, state)
        pair = shifted(as_sent(state[1]), "blk", 1)
        sums = jax.tree.map(
            lambda part, own: part.astype(own.dtype), from_behind(as_sent(sums), "blk", 1), sums
        )
        return (local, pair, sums)

    zero_rows = jnp.zeros(queries.shape, jnp.float32)
    zero_mixes = jnp.zeros(premix.shape, jnp.float32)
    state = lax.fori_loop(
        0,
        count - 1,
        keys_advance,
        ((zero_rows, zero_mixes, zero_mixes), (keys, values), (zero_rows, zero_rows)),
    )
    local, sums = visit(count - 1, state)
    sums = jax.tree.map(
        lambda part, own: part.astype(own.dtype), from_behind(as_sent(sums), "blk", 1), sums
    )
    return (local[0], sums[0], sums[1], local[1], local[2])


def on_device(
    inputs,
    lengths,
    prenorm,
    midnorm,
    query_proj,
    key_proj,
    value_proj,
    output_proj,
    premix,
    postmix,
    inner_proj,
    outer_proj,
    cotangent,
):
    gathered = (
        lax.all_gather(prenorm, ("blk", "dp"), axis=0, tiled=True),
        lax.all_gather(midnorm, ("blk", "dp"), axis=0, tiled=True),
        lax.all_gather(query_proj, ("blk", "dp"), axis=0, tiled=True),
        lax.all_gather(key_proj, ("blk", "dp"), axis=0, tiled=True),
        lax.all_gather(value_proj, ("blk", "dp"), axis=0, tiled=True),
        lax.all_gather(output_proj, ("blk", "dp"), axis=0, tiled=True),
        lax.all_gather(inner_proj, ("blk", "dp"), axis=0, tiled=True),
        lax.all_gather(outer_proj, ("blk", "dp"), axis=0, tiled=True),
    )
    gain_first = gathered[0].astype(jnp.float32)
    gain_second = gathered[1].astype(jnp.float32)
    query_w, key_w, value_w, output_w, inner_w, outer_w = gathered[2:]
    rows, width, model = inputs.shape
    heads = premix.shape[0]
    head_size = model // heads
    place = lax.axis_index("blk")
    residual = inputs.astype(jnp.float32)
    normed_first, first_back = jax.vjp(normalize, residual, gain_first)
    normed_low = normed_first.astype(jnp.bfloat16)

    def project(weight):
        made = jnp.einsum("rtd,de->rte", normed_low, weight, preferred_element_type=jnp.float32)
        return made.astype(jnp.bfloat16).reshape(rows, width, heads, head_size)

    queries = project(query_w)
    keys = project(key_w)
    values = project(value_w)

    def beside_all(pair, visit, carry):
        return key_cycle(pair, visit, carry)

    def stats_visit(carry, pair, key_block):
        peak, total = carry
        allowed = block_mask(lengths, place, key_block, width)
        unused, logits = block_logits(queries, pair[0], premix, allowed)
        fresh = jnp.maximum(peak, jnp.max(logits, axis=-1))
        exponents = jnp.where(allowed, jnp.exp(logits - fresh[..., None]), 0.0)
        return (fresh, total * jnp.exp(peak - fresh) + jnp.sum(exponents, axis=-1))

    start_peak = jnp.full((rows, heads, width), NEGATIVE, jnp.float32)
    start_total = jnp.zeros((rows, heads, width), jnp.float32)
    peak, total = beside_all((keys,), stats_visit, (start_peak, start_total))
    log_total = peak + jnp.log(total)

    def output_visit(carry, pair, key_block):
        allowed = block_mask(lengths, place, key_block, width)
        unused, logits = block_logits(queries, pair[0], premix, allowed)
        softmax_out = jnp.where(allowed, jnp.exp(logits - log_total[..., None]), 0.0)
        mixed = jnp.einsum("hk,rhij->rkij", postmix, softmax_out, precision=HIGH).astype(
            jnp.bfloat16
        )
        return carry + jnp.einsum(
            "rkij,rjkd->rikd", mixed, pair[1], preferred_element_type=jnp.float32
        )

    attended = beside_all(
        (keys, values), output_visit, jnp.zeros((rows, width, heads, head_size), jnp.float32)
    )
    joined = attended.astype(jnp.bfloat16).reshape(rows, width, model)
    middle = residual + jnp.einsum(
        "rtd,de->rte", joined, output_w, preferred_element_type=jnp.float32
    )
    positions = place * width + jnp.arange(width, dtype=jnp.int32)
    valid = (positions[None, :] < lengths[:, None]).astype(jnp.float32)[..., None]
    upgrad = cotangent.astype(jnp.float32) * valid

    def feed_row(totals, item):
        middle_row, grad_row, valid_row = item
        normed_mid, mid_back = jax.vjp(normalize, middle_row, gain_second)
        second = normed_mid.astype(jnp.bfloat16)
        inner = jnp.dot(second, inner_w, preferred_element_type=jnp.float32)
        activated, act_back = jax.vjp(smooth, inner)
        hidden = activated.astype(jnp.bfloat16)
        outer = jnp.dot(hidden, outer_w, preferred_element_type=jnp.float32)
        result = (valid_row * (middle_row + outer)).astype(jnp.bfloat16)
        grad_cast = grad_row.astype(jnp.bfloat16)
        outer_grad = totals[1] + jnp.einsum(
            "tf,td->fd", hidden, grad_cast, preferred_element_type=jnp.float32
        )
        hidden_grad = jnp.einsum(
            "td,fd->tf", grad_cast, outer_w, preferred_element_type=jnp.float32
        )
        inner_cast = act_back(hidden_grad)[0].astype(jnp.bfloat16)
        inner_grad = totals[0] + jnp.einsum(
            "td,tf->df", second, inner_cast, preferred_element_type=jnp.float32
        )
        second_grad = jnp.einsum(
            "tf,df->td", inner_cast, inner_w, preferred_element_type=jnp.float32
        )
        middle_part, gain_part = mid_back(second_grad)
        return ((inner_grad, outer_grad, totals[2] + gain_part), (result, grad_row + middle_part))

    start_totals = (
        jnp.zeros(inner_w.shape, jnp.float32),
        jnp.zeros(outer_w.shape, jnp.float32),
        jnp.zeros(gain_second.shape, jnp.float32),
    )
    ffn_totals, (outputs, middle_grad) = lax.scan(feed_row, start_totals, (middle, upgrad, valid))
    middle_cast = middle_grad.astype(jnp.bfloat16)
    output_grad = jnp.einsum("rtd,rte->de", joined, middle_cast, preferred_element_type=jnp.float32)
    upstream = jnp.einsum("rte,de->rtd", middle_cast, output_w, preferred_element_type=jnp.float32)
    upstream = upstream.astype(jnp.bfloat16).reshape(rows, width, heads, head_size)

    def dot_visit(carry, pair, key_block):
        allowed = block_mask(lengths, place, key_block, width)
        unused, logits = block_logits(queries, pair[0], premix, allowed)
        softmax_out = jnp.where(allowed, jnp.exp(logits - log_total[..., None]), 0.0)
        mixed_grad = jnp.einsum(
            "rikd,rjkd->rkij", upstream, pair[1], preferred_element_type=jnp.float32
        )
        prob_grad = jnp.einsum("hk,rkij->rhij", postmix, mixed_grad, precision=HIGH)
        return carry + jnp.sum(softmax_out * prob_grad, axis=-1)

    dot_sum = beside_all((keys, values), dot_visit, jnp.zeros((rows, heads, width), jnp.float32))
    query_grad, key_grad, value_grad, pre_grad, post_grad = keys_circle(
        queries, upstream, log_total, dot_sum, keys, values, lengths, premix, postmix
    )
    query_cast = query_grad.astype(jnp.bfloat16).reshape(rows, width, model)
    key_cast = key_grad.astype(jnp.bfloat16).reshape(rows, width, model)
    value_cast = value_grad.astype(jnp.bfloat16).reshape(rows, width, model)
    query_wgrad = jnp.einsum(
        "rtd,rte->de", normed_low, query_cast, preferred_element_type=jnp.float32
    )
    key_wgrad = jnp.einsum("rtd,rte->de", normed_low, key_cast, preferred_element_type=jnp.float32)
    value_wgrad = jnp.einsum(
        "rtd,rte->de", normed_low, value_cast, preferred_element_type=jnp.float32
    )
    normed_grad = jnp.einsum("rte,de->rtd", query_cast, query_w, preferred_element_type=jnp.float32)
    normed_grad = normed_grad + jnp.einsum(
        "rte,de->rtd", key_cast, key_w, preferred_element_type=jnp.float32
    )
    normed_grad = normed_grad + jnp.einsum(
        "rte,de->rtd", value_cast, value_w, preferred_element_type=jnp.float32
    )
    input_part, gain_first_grad = first_back(normed_grad)
    grad_inputs = (middle_grad + input_part).astype(jnp.bfloat16)
    summed = (
        lax.psum_scatter(gain_first_grad, ("blk", "dp"), scatter_dimension=0, tiled=True),
        lax.psum_scatter(ffn_totals[2], ("blk", "dp"), scatter_dimension=0, tiled=True),
        lax.psum_scatter(query_wgrad, ("blk", "dp"), scatter_dimension=0, tiled=True),
        lax.psum_scatter(key_wgrad, ("blk", "dp"), scatter_dimension=0, tiled=True),
        lax.psum_scatter(value_wgrad, ("blk", "dp"), scatter_dimension=0, tiled=True),
        lax.psum_scatter(output_grad, ("blk", "dp"), scatter_dimension=0, tiled=True),
        lax.psum_scatter(ffn_totals[0], ("blk", "dp"), scatter_dimension=0, tiled=True),
        lax.psum_scatter(ffn_totals[1], ("blk", "dp"), scatter_dimension=0, tiled=True),
    )
    mixes = lax.psum((pre_grad, post_grad), ("blk", "dp"))
    return (
        outputs,
        grad_inputs,
        summed[0],
        summed[1],
        summed[2],
        summed[3],
        summed[4],
        summed[5],
        mixes[0],
        mixes[1],
        summed[6],
        summed[7],
    )


def solution(mesh):
    in_specs = (
        P("dp", "blk", None),
        P("dp"),
        P(("blk", "dp")),
        P(("blk", "dp")),
        P(("blk", "dp"), None),
        P(("blk", "dp"), None),
        P(("blk", "dp"), None),
        P(("blk", "dp"), None),
        P(),
        P(),
        P(("blk", "dp"), None),
        P(("blk", "dp"), None),
        P("dp", "blk", None),
    )
    out_specs = (
        P("dp", "blk", None),
        P("dp", "blk", None),
        P(("blk", "dp")),
        P(("blk", "dp")),
        P(("blk", "dp"), None),
        P(("blk", "dp"), None),
        P(("blk", "dp"), None),
        P(("blk", "dp"), None),
        P(),
        P(),
        P(("blk", "dp"), None),
        P(("blk", "dp"), None),
    )
    return jax.shard_map(
        on_device, mesh=mesh, in_specs=in_specs, out_specs=out_specs, check_vma=False
    )
```

profile of v0, /device:TPU:0, one launch (start us, length us, event | category | flops | bytes accessed | tf_op | source)
XLA Modules:
  0.0 1496.3 jit_solution(17648627280104886)
XLA Ops:
  13.0 42.1 %all-reduce.5 = (bf16[768]{0:T(1024)(128)(2,1)S(1)}, bf16[768]{0:T(1024)(128)(2,1)S(1)}) all-reduce(bf16[768]{0:T(1024)(128)(2,1)S(1)} %dynamic-update-slice, bf16[768]{0:T(1024)(128)(2,1)S(1)} %dynamic-update-slice.1), channel_id=1, replica_groups=mesh['blk'=8,'dp'=4] {'blk','dp'}, use_global_device_ids=true, to_apply=%add | all-reduce | flops 1536 | bytes 6144
  61.8 5.9 all-gather.7.cloned.1.call-done
  69.8 53.8 %all-gather.11.cloned.1.call-done = bf16[768,768]{1,0:T(8,128)(2,1)} async-done(((bf16[24,768]{1,0:T(8,128)(2,1)}), bf16[768,768]{1,0:T(8,128)(2,1)}) %all-gather.11.cloned.1.call-update) | async-done | bytes 1179664 | tf_op jit(solution)/shard_map/all_gather | solution.py:164
  125.6 68.5 %while.115 = (s32[]{:T(128)}, f32[2,12,128]{1,2,0:T(8,128)S(1)}, f32[2,12,128]{1,2,0:T(8,128)S(1)}, bf16[2,128,12,64]{1,3,2,0:T(8,128)(2,1)S(1)}, s32[]{:T(128)}...) while((s32[]{:T(128)}, f32[2,12,128]{1,2,0:T(8,128)S(1)}, ...), condition=%wide.region_6.7_spmd, body=%wide.region_1.6_spmd.sunk | while | flops 109763072 | bytes 9731959 | solution.py:97
  128.6 7.4 conditional.17
  142.2 8.1 collective-permute-start
  152.6 6.7 collective-permute-start
  161.6 10.9 collective-permute-start
  174.8 7.8 collective-permute-start
  184.8 7.8 collective-permute-start
  197.9 123.7 %while.116 = (s32[]{:T(128)}, f32[2,128,12,64]{1,3,2,0:T(8,128)S(1)}, bf16[2,128,12,64]{1,3,2,0:T(8,128)(2,1)S(1)}, bf16[2,128,12,64]{1,3,2,0:T(8,128)(2,1)S(1)}...) while((s32[]{:T(128)}, ...), condition=%wide.region_14.15_spmd, body=%wide.region_11.14_spmd.sunk | while | flops 216121856 | bytes 15450591 | solution.py:97
  198.6 7.8 collective-permute-start.1
  211.5 10.5 conditional.18
  235.2 11.0 collective-permute-start.1
  251.1 8.0 collective-permute-start.1
  267.0 11.2 collective-permute-start.1
  285.4 15.4 %collective-permute-start.1 = (bf16[2,128,12,64]{1,3,2,0:T(8,128)(2,1)}, bf16[2,128,12,64]{1,3,2,0:T(8,128)(2,1)S(1)}, u32[]{:S(2)}, u32[]{:S(2)}) collective-permute-start(bf16[2,128,12,64]{1,3,2,0:T(8,128)(2,1)} %copy.364), channel_id=1, source_target_pairs={{0,4},{4,8},{8,12},{12,16},{16,20},{20,24},{24,28},{1,5},{5,9},{9,... | collective-permute-start | bytes 1179656 | tf_op jit(solution)/shard_map/while/body/eval_jaxpr/ppermute | solution.py:22
  308.1 7.0 collective-permute-start.1
  324.7 46.3 %all-gather.17.cloned.1.call-done = bf16[768,3072]{1,0:T(8,128)(2,1)} async-done(((bf16[24,3072]{1,0:T(8,128)(2,1)}), bf16[768,3072]{1,0:T(8,128)(2,1)}) %all-gather.17.cloned.1.call-update) | async-done | bytes 4718608 | tf_op jit(solution)/shard_map/all_gather | solution.py:168
  371.0 54.9 %while.118 = (s32[]{:T(128)}, f32[768,3072]{1,0:T(8,128)}, f32[3072,768]{1,0:T(8,128)}, f32[768]{0:T(1024)}, bf16[2,128,768]{2,1,0:T(8,128)(2,1)}, /*index=5*/f3...) while((s32[]{:T(128)}, f32[768,3072]{1,0:T(8,128)}, ...), condition=%wide.region_21.22_spmd.clone, body=%wide.region_17.21_spmd.clone.sunk | while | flops 3650520320 | bytes 126488592 | solution.py:259
  378.3 6.0 select_add_fusion.6
  402.3 9.0 select_add_fusion.6
  411.4 9.2 select_add_fusion.7
  434.1 109.4 %while.117 = (s32[]{:T(128)}, f32[2,12,128]{1,2,0:T(8,128)S(1)}, bf16[2,128,12,64]{1,3,2,0:T(8,128)(2,1)S(1)}, bf16[2,128,12,64]{1,3,2,0:T(8,128)(2,1)S(1)}, s32...) while((s32[]{:T(128)}, f32[2,12,128]{1,2,0:T(8,128)S(1)}, ...), condition=%wide.region_26.27_spmd, body=%wide.region_22.26_spmd.sunk | while | flops 216318464 | bytes 15892975 | solution.py:97
  441.0 11.8 conditional.19
  462.1 12.5 collective-permute-start.3
  479.9 11.1 collective-permute-start.3
  498.4 8.0 collective-permute-start.3
  513.7 9.0 collective-permute-start.3
  530.0 6.9 collective-permute-start.3
  544.8 320.9 %while.119 = (s32[]{:T(128)}, f32[2,128,12,64]{1,3,2,0:T(8,128)S(1)}, f32[12,12]{1,0:T(8,128)}, f32[12,12]{1,0:T(8,128)}, bf16[2,128,12,64]{1,3,2,0:T(8,128)(2,1...) while((s32[]{:T(128)}, ...), condition=%wide.region_33.34_spmd.clone, body=%wide.region_30.33_spmd.clone.sunk | while | flops 596755200 | bytes 47867304 | solution.py:133
  546.1 23.9 %conditional.20 = ((f32[2,128,12,64]{1,3,2,0:T(8,128)S(1)}, f32[12,12]{1,0:T(8,128)}, f32[12,12]{1,0:T(8,128)}, f32[2,128,12,64]{1,3,2,0:T(8,128)S(1)}, f32[2,128,12,64]{1,3,2,0:T(8,128)S(1)})) conditional(s32[]{:T(128)} %convert_element_type.353, (f32[2,128,12,64]{1,3,2,0:T(8,128)S(1)}, f32[12,12]{1,0:T(8,128)}, f32[12,12]{1,0:T(8,128)}, ...), branch_computations={%region_31.31_spmd, %region_32.32_spmd} | conditional | flops 595575552 | bytes 32039652 | solution.py:121
  599.4 23.6 %collective-permute-start.7 = (bf16[2,128,12,64]{1,3,2,0:T(8,128)(2,1)}, bf16[2,128,12,64]{1,3,2,0:T(8,128)(2,1)S(1)}, u32[]{:S(2)}, u32[]{:S(2)}) collective-permute-start(bf16[2,128,12,64]{1,3,2,0:T(8,128)(2,1)} %convert_element_type.354), channel_id=1, source_target_pairs={{28,0},{0,4},{4,8},{8,12},{12,16},{16,20},{20,24},{24,28},{29,1},{... | collective-permute-start | bytes 1179656 | tf_op jit(solution)/shard_map/while/body/eval_jaxpr/ppermute | solution.py:28
  647.6 26.3 %collective-permute-start.8 = (bf16[2,128,12,64]{1,3,2,0:T(8,128)(2,1)}, bf16[2,128,12,64]{1,3,2,0:T(8,128)(2,1)}, u32[]{:S(2)}, u32[]{:S(2)}) collective-permute-start(bf16[2,128,12,64]{1,3,2,0:T(8,128)(2,1)} %convert_element_type.356), channel_id=1, source_target_pairs={{28,0},{0,4},{4,8},{8,12},{12,16},{16,20},{20,24},{24,28},{29,1},{... | collective-permute-start | bytes 1179656 | tf_op jit(solution)/shard_map/while/body/eval_jaxpr/ppermute | solution.py:28
  673.9 5.5 collective-permute-start.5
  698.0 29.4 %collective-permute-start.5 = (bf16[2,128,12,64]{1,3,2,0:T(8,128)(2,1)S(1)}, bf16[2,128,12,64]{1,3,2,0:T(8,128)(2,1)S(1)}, u32[]{:S(2)}, u32[]{:S(2)}) collective-permute-start(bf16[2,128,12,64]{1,3,2,0:T(8,128)(2,1)S(1)} %copy.416), channel_id=1, source_target_pairs={{0,4},{4,8},{8,12},{12,16},{16,20},{20,24},{24,28},{1,5},{5,9},{9,... | collective-permute-start | bytes 1179656 | tf_op jit(solution)/shard_map/while/body/eval_jaxpr/ppermute | solution.py:22
  751.4 29.1 %collective-permute-start.6 = (bf16[2,128,12,64]{1,3,2,0:T(8,128)(2,1)}, bf16[2,128,12,64]{1,3,2,0:T(8,128)(2,1)S(1)}, u32[]{:S(2)}, u32[]{:S(2)}) collective-permute-start(bf16[2,128,12,64]{1,3,2,0:T(8,128)(2,1)} %copy.417), channel_id=1, source_target_pairs={{0,4},{4,8},{8,12},{12,16},{16,20},{20,24},{24,28},{1,5},{5,9},{9,... | collective-permute-start | bytes 1179656 | tf_op jit(solution)/shard_map/while/body/eval_jaxpr/ppermute | solution.py:22
  804.6 7.5 collective-permute-done.7
  821.6 11.5 collective-permute-start.7
  845.6 13.5 collective-permute-done.7
  873.3 33.4 %collective-permute-done.10 = bf16[2,128,12,64]{1,3,2,0:T(8,128)(2,1)S(1)} collective-permute-done((bf16[2,128,12,64]{1,3,2,0:T(8,128)(2,1)S(1)}, bf16[2,128,12,64]{1,3,2,0:T(8,128)(2,1)S(1)}, u32[]{:S(2)}, u32[]{:S(2)}) %collective-permute-start.10) | collective-permute-done | bytes 393248 | tf_op jit(solution)/shard_map/ppermute | solution.py:28
  909.0 8.1 collective-permute-done.9
  924.5 40.1 %all-reduce.4 = (f32[768]{0:T(1024)S(1)}, f32[768]{0:T(1024)S(1)}, f32[12,12]{1,0:T(8,128)}, f32[12,12]{1,0:T(8,128)}) all-reduce(f32[768]{0:T(1024)S(1)} %get-tuple-element.1916, f32[768]{0:T(1024)S(1)} %copy-done.45, f32[12,12]{1,0:T(8,128)S(1)} %copy-done.35, ...), channel_id=2, replica_groups=mesh['blk'=8,'dp'=4] {'blk','dp'}, use_global_device_ids=true, to_apply=%region_38.39.clone | all-reduce | flops 1824 | bytes 14592
  966.8 30.9 %reduce-scatter.7.cloned.1.call-done = f32[24,768]{1,0:T(8,128)} async-done(((f32[768,768]{1,0:T(8,128)}), f32[24,768]{1,0:T(8,128)}) %reduce-scatter.7.cloned.1.call-update) | async-done | bytes 73744 | tf_op jit(solution)/shard_map/reduce_scatter | solution.py:301
  997.7 103.9 %reduce-scatter.11.cloned.1.call-done = f32[24,768]{1,0:T(8,128)} async-done(((f32[768,768]{1,0:T(8,128)}), f32[24,768]{1,0:T(8,128)}) %reduce-scatter.11.cloned.1.call-update) | async-done | bytes 73744 | tf_op jit(solution)/shard_map/reduce_scatter | solution.py:303
  1101.5 104.7 %reduce-scatter.9.cloned.1.call-done = f32[24,768]{1,0:T(8,128)} async-done(((f32[768,768]{1,0:T(8,128)}), f32[24,768]{1,0:T(8,128)}) %reduce-scatter.9.cloned.1.call-update) | async-done | bytes 73744 | tf_op jit(solution)/shard_map/reduce_scatter | solution.py:302
  1206.2 141.0 %reduce-scatter.15.cloned.1.call-done = f32[24,3072]{1,0:T(8,128)} async-done(((f32[768,3072]{1,0:T(8,128)}), f32[24,3072]{1,0:T(8,128)}) %reduce-scatter.15.cloned.1.call-update) | async-done | bytes 294928 | tf_op jit(solution)/shard_map/reduce_scatter | solution.py:305
  1347.2 142.0 %reduce-scatter.17.cloned.1.call-done = f32[96,768]{1,0:T(8,128)} async-done(((f32[3072,768]{1,0:T(8,128)}), f32[96,768]{1,0:T(8,128)}) %reduce-scatter.17.cloned.1.call-update) | async-done | bytes 294928 | tf_op jit(solution)/shard_map/reduce_scatter | solution.py:306
  (517 shorter events, 408.0 us)
Async XLA Ops:
  7.2 60.5 %all-gather.7.cloned.1.call-start = ((), (), s32[]{:S(2)}) async-start(), calls=%async_computation.6 | async-start | bytes 1216512 | tf_op jit(solution)/shard_map/all_gather | solution.py:165
  7.9 115.7 %all-gather.11.cloned.1.call-start = ((), (), s32[]{:S(2)}) async-start(), calls=%async_computation.8 | async-start | bytes 1216512 | tf_op jit(solution)/shard_map/all_gather | solution.py:164
  8.7 185.4 %all-gather.9.cloned.1.call-start = ((), (), s32[]{:S(2)}) async-start(), calls=%async_computation.7 | async-start | bytes 1216512 | tf_op jit(solution)/shard_map/all_gather | solution.py:166
  9.4 313.4 %all-gather.13.cloned.1.call-start = ((), (), s32[]{:S(2)}) async-start(), calls=%async_computation.9 | async-start | bytes 1216512 | tf_op jit(solution)/shard_map/all_gather | solution.py:167
  10.0 314.7 %all-gather.15.cloned.1.call-start = ((), (), s32[]{:S(2)}) async-start(), calls=%async_computation.10 | async-start | bytes 4866048 | tf_op jit(solution)/shard_map/all_gather | solution.py:169
  10.6 360.4 %all-gather.17.cloned.1.call-start = ((), (), s32[]{:S(2)}) async-start(), calls=%async_computation.11 | async-start | bytes 4866048 | tf_op jit(solution)/shard_map/all_gather | solution.py:168
  11.1 955.6 %reduce-scatter.13.cloned.1.call-start = ((), (), s32[]{:S(2)}) async-start(), calls=%async_computation.15 | async-start | bytes 2433024 | tf_op jit(solution)/shard_map/reduce_scatter | solution.py:304
  198.6 23.4 %collective-permute-start.1 = (bf16[2,128,12,64]{1,3,2,0:T(8,128)(2,1)}, bf16[2,128,12,64]{1,3,2,0:T(8,128)(2,1)S(1)}, u32[]{:S(2)}, u32[]{:S(2)}) collective-permute-start(bf16[2,128,12,64]{1,3,2,0:T(8,128)(2,1)} %copy.364), channel_id=1, source_target_pairs={{0,4},{4,8},{8,12},{12,16},{16,20},{20,24},{24,28},{1,5},{5,9},{9,... | collective-permute-start | bytes 1179656 | tf_op jit(solution)/shard_map/while/body/eval_jaxpr/ppermute | solution.py:22
  207.2 14.8 collective-permute-start.2
  235.2 13.7 collective-permute-start.1
  251.1 13.7 collective-permute-start.1
  267.0 16.2 %collective-permute-start.1 = (bf16[2,128,12,64]{1,3,2,0:T(8,128)(2,1)}, bf16[2,128,12,64]{1,3,2,0:T(8,128)(2,1)S(1)}, u32[]{:S(2)}, u32[]{:S(2)}) collective-permute-start(bf16[2,128,12,64]{1,3,2,0:T(8,128)(2,1)} %copy.364), channel_id=1, source_target_pairs={{0,4},{4,8},{8,12},{12,16},{16,20},{20,24},{24,28},{1,5},{5,9},{9,... | collective-permute-start | bytes 1179656 | tf_op jit(solution)/shard_map/while/body/eval_jaxpr/ppermute | solution.py:22
  285.4 20.4 %collective-permute-start.1 = (bf16[2,128,12,64]{1,3,2,0:T(8,128)(2,1)}, bf16[2,128,12,64]{1,3,2,0:T(8,128)(2,1)S(1)}, u32[]{:S(2)}, u32[]{:S(2)}) collective-permute-start(bf16[2,128,12,64]{1,3,2,0:T(8,128)(2,1)} %copy.364), channel_id=1, source_target_pairs={{0,4},{4,8},{8,12},{12,16},{16,20},{20,24},{24,28},{1,5},{5,9},{9,... | collective-permute-start | bytes 1179656 | tf_op jit(solution)/shard_map/while/body/eval_jaxpr/ppermute | solution.py:22
  429.1 568.6 %reduce-scatter.7.cloned.1.call-start = ((), (), s32[]{:S(2)}) async-start(), calls=%async_computation.12 | async-start | bytes 2433024 | tf_op jit(solution)/shard_map/reduce_scatter | solution.py:301
  434.9 17.9 %collective-permute-start.3 = (bf16[2,128,12,64]{1,3,2,0:T(8,128)(2,1)}, bf16[2,128,12,64]{1,3,2,0:T(8,128)(2,1)S(1)}, u32[]{:S(2)}, u32[]{:S(2)}) collective-permute-start(bf16[2,128,12,64]{1,3,2,0:T(8,128)(2,1)} %copy.396), channel_id=1, source_target_pairs={{0,4},{4,8},{8,12},{12,16},{16,20},{20,24},{24,28},{1,5},{5,9},{9,... | collective-permute-start | bytes 1179656 | tf_op jit(solution)/shard_map/while/body/eval_jaxpr/ppermute | solution.py:22
  437.9 15.0 %collective-permute-start.4 = (bf16[2,128,12,64]{1,3,2,0:T(8,128)(2,1)}, bf16[2,128,12,64]{1,3,2,0:T(8,128)(2,1)S(1)}, u32[]{:S(2)}, u32[]{:S(2)}) collective-permute-start(bf16[2,128,12,64]{1,3,2,0:T(8,128)(2,1)} %copy.397), channel_id=1, source_target_pairs={{0,4},{4,8},{8,12},{12,16},{16,20},{20,24},{24,28},{1,5},{5,9},{9,... | collective-permute-start | bytes 1179656 | tf_op jit(solution)/shard_map/while/body/eval_jaxpr/ppermute | solution.py:22
  462.1 15.6 %collective-permute-start.3 = (bf16[2,128,12,64]{1,3,2,0:T(8,128)(2,1)}, bf16[2,128,12,64]{1,3,2,0:T(8,128)(2,1)S(1)}, u32[]{:S(2)}, u32[]{:S(2)}) collective-permute-start(bf16[2,128,12,64]{1,3,2,0:T(8,128)(2,1)} %copy.396), channel_id=1, source_target_pairs={{0,4},{4,8},{8,12},{12,16},{16,20},{20,24},{24,28},{1,5},{5,9},{9,... | collective-permute-start | bytes 1179656 | tf_op jit(solution)/shard_map/while/body/eval_jaxpr/ppermute | solution.py:22
  479.9 16.2 %collective-permute-start.3 = (bf16[2,128,12,64]{1,3,2,0:T(8,128)(2,1)}, bf16[2,128,12,64]{1,3,2,0:T(8,128)(2,1)S(1)}, u32[]{:S(2)}, u32[]{:S(2)}) collective-permute-start(bf16[2,128,12,64]{1,3,2,0:T(8,128)(2,1)} %copy.396), channel_id=1, source_target_pairs={{0,4},{4,8},{8,12},{12,16},{16,20},{20,24},{24,28},{1,5},{5,9},{9,... | collective-permute-start | bytes 1179656 | tf_op jit(solution)/shard_map/while/body/eval_jaxpr/ppermute | solution.py:22
  513.7 14.0 collective-permute-start.3
  570.9 19.0 %collective-permute-start.7 = (bf16[2,128,12,64]{1,3,2,0:T(8,128)(2,1)}, bf16[2,128,12,64]{1,3,2,0:T(8,128)(2,1)S(1)}, u32[]{:S(2)}, u32[]{:S(2)}) collective-permute-start(bf16[2,128,12,64]{1,3,2,0:T(8,128)(2,1)} %convert_element_type.354), channel_id=1, source_target_pairs={{28,0},{0,4},{4,8},{8,12},{12,16},{16,20},{20,24},{24,28},{29,1},{... | collective-permute-start | bytes 1179656 | tf_op jit(solution)/shard_map/while/body/eval_jaxpr/ppermute | solution.py:28
  576.7 17.5 %collective-permute-start.8 = (bf16[2,128,12,64]{1,3,2,0:T(8,128)(2,1)}, bf16[2,128,12,64]{1,3,2,0:T(8,128)(2,1)}, u32[]{:S(2)}, u32[]{:S(2)}) collective-permute-start(bf16[2,128,12,64]{1,3,2,0:T(8,128)(2,1)} %convert_element_type.356), channel_id=1, source_target_pairs={{28,0},{0,4},{4,8},{8,12},{12,16},{16,20},{20,24},{24,28},{29,1},{... | collective-permute-start | bytes 1179656 | tf_op jit(solution)/shard_map/while/body/eval_jaxpr/ppermute | solution.py:28
  579.1 17.1 %collective-permute-start.5 = (bf16[2,128,12,64]{1,3,2,0:T(8,128)(2,1)S(1)}, bf16[2,128,12,64]{1,3,2,0:T(8,128)(2,1)S(1)}, u32[]{:S(2)}, u32[]{:S(2)}) collective-permute-start(bf16[2,128,12,64]{1,3,2,0:T(8,128)(2,1)S(1)} %copy.416), channel_id=1, source_target_pairs={{0,4},{4,8},{8,12},{12,16},{16,20},{20,24},{24,28},{1,5},{5,9},{9,... | collective-permute-start | bytes 1179656 | tf_op jit(solution)/shard_map/while/body/eval_jaxpr/ppermute | solution.py:22
  599.4 37.2 %collective-permute-start.7 = (bf16[2,128,12,64]{1,3,2,0:T(8,128)(2,1)}, bf16[2,128,12,64]{1,3,2,0:T(8,128)(2,1)S(1)}, u32[]{:S(2)}, u32[]{:S(2)}) collective-permute-start(bf16[2,128,12,64]{1,3,2,0:T(8,128)(2,1)} %convert_element_type.354), channel_id=1, source_target_pairs={{28,0},{0,4},{4,8},{8,12},{12,16},{16,20},{20,24},{24,28},{29,1},{... | collective-permute-start | bytes 1179656 | tf_op jit(solution)/shard_map/while/body/eval_jaxpr/ppermute | solution.py:28
  623.8 13.8 collective-permute-start.8
  626.2 13.5 collective-permute-start.5
  642.8 41.8 %collective-permute-start.7 = (bf16[2,128,12,64]{1,3,2,0:T(8,128)(2,1)}, bf16[2,128,12,64]{1,3,2,0:T(8,128)(2,1)S(1)}, u32[]{:S(2)}, u32[]{:S(2)}) collective-permute-start(bf16[2,128,12,64]{1,3,2,0:T(8,128)(2,1)} %convert_element_type.354), channel_id=1, source_target_pairs={{28,0},{0,4},{4,8},{8,12},{12,16},{16,20},{20,24},{24,28},{29,1},{... | collective-permute-start | bytes 1179656 | tf_op jit(solution)/shard_map/while/body/eval_jaxpr/ppermute | solution.py:28
  647.6 37.9 %collective-permute-start.8 = (bf16[2,128,12,64]{1,3,2,0:T(8,128)(2,1)}, bf16[2,128,12,64]{1,3,2,0:T(8,128)(2,1)}, u32[]{:S(2)}, u32[]{:S(2)}) collective-permute-start(bf16[2,128,12,64]{1,3,2,0:T(8,128)(2,1)} %convert_element_type.356), channel_id=1, source_target_pairs={{28,0},{0,4},{4,8},{8,12},{12,16},{16,20},{20,24},{24,28},{29,1},{... | collective-permute-start | bytes 1179656 | tf_op jit(solution)/shard_map/while/body/eval_jaxpr/ppermute | solution.py:28
  673.9 13.7 collective-permute-start.5
  690.8 41.8 %collective-permute-start.7 = (bf16[2,128,12,64]{1,3,2,0:T(8,128)(2,1)}, bf16[2,128,12,64]{1,3,2,0:T(8,128)(2,1)S(1)}, u32[]{:S(2)}, u32[]{:S(2)}) collective-permute-start(bf16[2,128,12,64]{1,3,2,0:T(8,128)(2,1)} %convert_element_type.354), channel_id=1, source_target_pairs={{28,0},{0,4},{4,8},{8,12},{12,16},{16,20},{20,24},{24,28},{29,1},{... | collective-permute-start | bytes 1179656 | tf_op jit(solution)/shard_map/while/body/eval_jaxpr/ppermute | solution.py:28
  695.6 37.9 %collective-permute-start.8 = (bf16[2,128,12,64]{1,3,2,0:T(8,128)(2,1)}, bf16[2,128,12,64]{1,3,2,0:T(8,128)(2,1)}, u32[]{:S(2)}, u32[]{:S(2)}) collective-permute-start(bf16[2,128,12,64]{1,3,2,0:T(8,128)(2,1)} %convert_element_type.356), channel_id=1, source_target_pairs={{28,0},{0,4},{4,8},{8,12},{12,16},{16,20},{20,24},{24,28},{29,1},{... | collective-permute-start | bytes 1179656 | tf_op jit(solution)/shard_map/while/body/eval_jaxpr/ppermute | solution.py:28
  698.0 37.6 %collective-permute-start.5 = (bf16[2,128,12,64]{1,3,2,0:T(8,128)(2,1)S(1)}, bf16[2,128,12,64]{1,3,2,0:T(8,128)(2,1)S(1)}, u32[]{:S(2)}, u32[]{:S(2)}) collective-permute-start(bf16[2,128,12,64]{1,3,2,0:T(8,128)(2,1)S(1)} %copy.416), channel_id=1, source_target_pairs={{0,4},{4,8},{8,12},{12,16},{16,20},{20,24},{24,28},{1,5},{5,9},{9,... | collective-permute-start | bytes 1179656 | tf_op jit(solution)/shard_map/while/body/eval_jaxpr/ppermute | solution.py:22
  738.8 41.8 %collective-permute-start.7 = (bf16[2,128,12,64]{1,3,2,0:T(8,128)(2,1)}, bf16[2,128,12,64]{1,3,2,0:T(8,128)(2,1)S(1)}, u32[]{:S(2)}, u32[]{:S(2)}) collective-permute-start(bf16[2,128,12,64]{1,3,2,0:T(8,128)(2,1)} %convert_element_type.354), channel_id=1, source_target_pairs={{28,0},{0,4},{4,8},{8,12},{12,16},{16,20},{20,24},{24,28},{29,1},{... | collective-permute-start | bytes 1179656 | tf_op jit(solution)/shard_map/while/body/eval_jaxpr/ppermute | solution.py:28
  743.6 37.9 %collective-permute-start.8 = (bf16[2,128,12,64]{1,3,2,0:T(8,128)(2,1)}, bf16[2,128,12,64]{1,3,2,0:T(8,128)(2,1)}, u32[]{:S(2)}, u32[]{:S(2)}) collective-permute-start(bf16[2,128,12,64]{1,3,2,0:T(8,128)(2,1)} %convert_element_type.356), channel_id=1, source_target_pairs={{28,0},{0,4},{4,8},{8,12},{12,16},{16,20},{20,24},{24,28},{29,1},{... | collective-permute-start | bytes 1179656 | tf_op jit(solution)/shard_map/while/body/eval_jaxpr/ppermute | solution.py:28
  746.0 37.6 %collective-permute-start.5 = (bf16[2,128,12,64]{1,3,2,0:T(8,128)(2,1)S(1)}, bf16[2,128,12,64]{1,3,2,0:T(8,128)(2,1)S(1)}, u32[]{:S(2)}, u32[]{:S(2)}) collective-permute-start(bf16[2,128,12,64]{1,3,2,0:T(8,128)(2,1)S(1)} %copy.416), channel_id=1, source_target_pairs={{0,4},{4,8},{8,12},{12,16},{16,20},{20,24},{24,28},{1,5},{5,9},{9,... | collective-permute-start | bytes 1179656 | tf_op jit(solution)/shard_map/while/body/eval_jaxpr/ppermute | solution.py:22
  751.4 32.1 %collective-permute-start.6 = (bf16[2,128,12,64]{1,3,2,0:T(8,128)(2,1)}, bf16[2,128,12,64]{1,3,2,0:T(8,128)(2,1)S(1)}, u32[]{:S(2)}, u32[]{:S(2)}) collective-permute-start(bf16[2,128,12,64]{1,3,2,0:T(8,128)(2,1)} %copy.417), channel_id=1, source_target_pairs={{0,4},{4,8},{8,12},{12,16},{16,20},{20,24},{24,28},{1,5},{5,9},{9,... | collective-permute-start | bytes 1179656 | tf_op jit(solution)/shard_map/while/body/eval_jaxpr/ppermute | solution.py:22
  786.7 25.3 %collective-permute-start.7 = (bf16[2,128,12,64]{1,3,2,0:T(8,128)(2,1)}, bf16[2,128,12,64]{1,3,2,0:T(8,128)(2,1)S(1)}, u32[]{:S(2)}, u32[]{:S(2)}) collective-permute-start(bf16[2,128,12,64]{1,3,2,0:T(8,128)(2,1)} %convert_element_type.354), channel_id=1, source_target_pairs={{28,0},{0,4},{4,8},{8,12},{12,16},{16,20},{20,24},{24,28},{29,1},{... | collective-permute-start | bytes 1179656 | tf_op jit(solution)/shard_map/while/body/eval_jaxpr/ppermute | solution.py:28
  791.5 24.8 %collective-permute-start.8 = (bf16[2,128,12,64]{1,3,2,0:T(8,128)(2,1)}, bf16[2,128,12,64]{1,3,2,0:T(8,128)(2,1)}, u32[]{:S(2)}, u32[]{:S(2)}) collective-permute-start(bf16[2,128,12,64]{1,3,2,0:T(8,128)(2,1)} %convert_element_type.356), channel_id=1, source_target_pairs={{28,0},{0,4},{4,8},{8,12},{12,16},{16,20},{20,24},{24,28},{29,1},{... | collective-permute-start | bytes 1179656 | tf_op jit(solution)/shard_map/while/body/eval_jaxpr/ppermute | solution.py:28
  793.9 24.5 %collective-permute-start.5 = (bf16[2,128,12,64]{1,3,2,0:T(8,128)(2,1)S(1)}, bf16[2,128,12,64]{1,3,2,0:T(8,128)(2,1)S(1)}, u32[]{:S(2)}, u32[]{:S(2)}) collective-permute-start(bf16[2,128,12,64]{1,3,2,0:T(8,128)(2,1)S(1)} %copy.416), channel_id=1, source_target_pairs={{0,4},{4,8},{8,12},{12,16},{16,20},{20,24},{24,28},{1,5},{5,9},{9,... | collective-permute-start | bytes 1179656 | tf_op jit(solution)/shard_map/while/body/eval_jaxpr/ppermute | solution.py:22
  799.4 19.0 %collective-permute-start.6 = (bf16[2,128,12,64]{1,3,2,0:T(8,128)(2,1)}, bf16[2,128,12,64]{1,3,2,0:T(8,128)(2,1)S(1)}, u32[]{:S(2)}, u32[]{:S(2)}) collective-permute-start(bf16[2,128,12,64]{1,3,2,0:T(8,128)(2,1)} %copy.417), channel_id=1, source_target_pairs={{0,4},{4,8},{8,12},{12,16},{16,20},{20,24},{24,28},{1,5},{5,9},{9,... | collective-permute-start | bytes 1179656 | tf_op jit(solution)/shard_map/while/body/eval_jaxpr/ppermute | solution.py:22
  821.6 37.6 %collective-permute-start.7 = (bf16[2,128,12,64]{1,3,2,0:T(8,128)(2,1)}, bf16[2,128,12,64]{1,3,2,0:T(8,128)(2,1)S(1)}, u32[]{:S(2)}, u32[]{:S(2)}) collective-permute-start(bf16[2,128,12,64]{1,3,2,0:T(8,128)(2,1)} %convert_element_type.354), channel_id=1, source_target_pairs={{28,0},{0,4},{4,8},{8,12},{12,16},{16,20},{20,24},{24,28},{29,1},{... | collective-permute-start | bytes 1179656 | tf_op jit(solution)/shard_map/while/body/eval_jaxpr/ppermute | solution.py:28
  833.9 29.6 %collective-permute-start.8 = (bf16[2,128,12,64]{1,3,2,0:T(8,128)(2,1)}, bf16[2,128,12,64]{1,3,2,0:T(8,128)(2,1)}, u32[]{:S(2)}, u32[]{:S(2)}) collective-permute-start(bf16[2,128,12,64]{1,3,2,0:T(8,128)(2,1)} %convert_element_type.356), channel_id=1, source_target_pairs={{28,0},{0,4},{4,8},{8,12},{12,16},{16,20},{20,24},{24,28},{29,1},{... | collective-permute-start | bytes 1179656 | tf_op jit(solution)/shard_map/while/body/eval_jaxpr/ppermute | solution.py:28
  836.2 29.3 %collective-permute-start.5 = (bf16[2,128,12,64]{1,3,2,0:T(8,128)(2,1)S(1)}, bf16[2,128,12,64]{1,3,2,0:T(8,128)(2,1)S(1)}, u32[]{:S(2)}, u32[]{:S(2)}) collective-permute-start(bf16[2,128,12,64]{1,3,2,0:T(8,128)(2,1)S(1)} %copy.416), channel_id=1, source_target_pairs={{0,4},{4,8},{8,12},{12,16},{16,20},{20,24},{24,28},{1,5},{5,9},{9,... | collective-permute-start | bytes 1179656 | tf_op jit(solution)/shard_map/while/body/eval_jaxpr/ppermute | solution.py:22
  840.4 25.1 %collective-permute-start.6 = (bf16[2,128,12,64]{1,3,2,0:T(8,128)(2,1)}, bf16[2,128,12,64]{1,3,2,0:T(8,128)(2,1)S(1)}, u32[]{:S(2)}, u32[]{:S(2)}) collective-permute-start(bf16[2,128,12,64]{1,3,2,0:T(8,128)(2,1)} %copy.417), channel_id=1, source_target_pairs={{0,4},{4,8},{8,12},{12,16},{16,20},{20,24},{24,28},{1,5},{5,9},{9,... | collective-permute-start | bytes 1179656 | tf_op jit(solution)/shard_map/while/body/eval_jaxpr/ppermute | solution.py:22
  873.1 228.5 %reduce-scatter.11.cloned.1.call-start = ((), (), s32[]{:S(2)}) async-start(), calls=%async_computation.14 | async-start | bytes 2433024 | tf_op jit(solution)/shard_map/reduce_scatter | solution.py:303
  873.2 33.5 %collective-permute-start.10 = (bf16[2,128,12,64]{1,3,2,0:T(8,128)(2,1)S(1)}, bf16[2,128,12,64]{1,3,2,0:T(8,128)(2,1)S(1)}, u32[]{:S(2)}, u32[]{:S(2)}) collective-permute-start(bf16[2,128,12,64]{1,3,2,0:T(8,128)(2,1)S(1)} %convert_element_type.236), channel_id=1, source_target_pairs={{28,0},{0,4},{4,8},{8,12},{12,16},{16,20},{20,24},{24,28},{29,1},{... | collective-permute-start | bytes 1179656 | tf_op jit(solution)/shard_map/ppermute | solution.py:28
  908.8 297.4 %reduce-scatter.9.cloned.1.call-start = ((), (), s32[]{:S(2)}) async-start(), calls=%async_computation.13 | async-start | bytes 2433024 | tf_op jit(solution)/shard_map/reduce_scatter | solution.py:302
  919.1 428.1 %reduce-scatter.15.cloned.1.call-start = ((), (), s32[]{:S(2)}) async-start(), calls=%async_computation.16 | async-start | bytes 9732096 | tf_op jit(solution)/shard_map/reduce_scatter | solution.py:305
  919.8 569.4 %reduce-scatter.17.cloned.1.call-start = ((), (), s32[]{:S(2)}) async-start(), calls=%async_computation.17 | async-start | bytes 9732096 | tf_op jit(solution)/shard_map/reduce_scatter | solution.py:306
  (103 other events, 1422.1 us)
Sparse Core Ops, SparseCore 0:
  10.8 56.8 all-gather.6
  70.5 53.0 all-gather.10
  126.4 53.3 all-gather.8
  182.4 53.2 all-gather.12
  238.3 67.3 all-gather.14
  308.4 62.5 all-gather.16
  429.2 101.9 reduce-scatter.12
  873.2 124.4 reduce-scatter.6
  1003.5 97.9 reduce-scatter.10
  1108.1 98.0 reduce-scatter.8
  1212.7 134.4 reduce-scatter.14
  1354.5 134.6 reduce-scatter.16
where the time goes:
time: 1510 us; the launch traced here: 1500 us
  waiting for transfers between devices  734 us (49%)
  starting transfers between devices  435 us (29%)
  matrix products  120 us (8%)
  blocking collectives  82.2 us (5%)
  other arithmetic  55 us (4%)
  local copies, waits for them, and re-layouts  48.4 us (3%)
    ppermute x49, starting transfers between devices, shifted(): lax.ppermute(value, axis, [(source, source + steps) for source in range(f...  337 us
    reduce_scatter x1, waiting for transfers between devices, on_device(): lax.psum_scatter(ffn_totals[1], ('blk', 'dp'), scatter_dimension=0, tiled...  142 us
    reduce_scatter x1, waiting for transfers between devices, on_device(): lax.psum_scatter(ffn_totals[0], ('blk', 'dp'), scatter_dimension=0, tiled...  141 us
    reduce_scatter x1, waiting for transfers between devices, on_device(): lax.psum_scatter(key_wgrad, ('blk', 'dp'), scatter_dimension=0, tiled=True)  105 us
    reduce_scatter x1, waiting for transfers between devices, on_device(): lax.psum_scatter(value_wgrad, ('blk', 'dp'), scatter_dimension=0, tiled=T...  104 us
    ppermute x16, starting transfers between devices, from_behind(): return lax.ppermute(block, axis, route)  96.7 us
    unnamed x2, blocking collectives  82.2 us
    ppermute x16, waiting for transfers between devices, from_behind(): return lax.ppermute(block, axis, route)  73.7 us
  transfers between devices with their start and end apart: 77, of which 34 were waited for; matrix products, arithmetic and copies ran while one was open for 11% of the time, Pallas kernels for 0%

commit v1 on v0

v1 whole, which is shorter than its diff:
```python
import jax
import jax.numpy as jnp
from jax import lax
from jax.experimental import pallas as pl
from jax.experimental.pallas import tpu as pltpu
from jax.sharding import PartitionSpec as P

EPSILON = 1e-06
GROUP = 4
HEADS = 12
f32 = jnp.float32
bf16 = jnp.bfloat16
CH=256

def dot(a,b,ca=1,cb=0):
    return lax.dot_general(a,b,(((ca,),(cb,)),((),())),preferred_element_type=f32)

def masked(tile, chunk, qb, width, fill):
    rows,lanes=tile.shape
    key=chunk*CH+lax.broadcasted_iota(jnp.int32,(rows,lanes),0)
    query=qb*width+lax.broadcasted_iota(jnp.int32,(rows,lanes),1)%width
    return jnp.where(key<=query,tile,fill)

def scaled_queries_t(vec_t, mix, out_ref, heads, width, size, scale, swap):
    for h in range(heads):
        for g in range(heads):
            m = mix[h,g] if swap else mix[g,h]
            out_ref[g*size:(g+1)*size, h*width:(h+1)*width] = (vec_t[g*size:(g+1)*size,:]*(m*scale)).astype(bf16)

def fwd_kernel(meta, premix, postmix, q_ref, k_ref, v_ref, joined_ref, ut_ref, lse_ref, qst, s_ref, acc, mx):
    width,model=q_ref.shape
    heads=HEADS; size=model//heads
    qb=meta[0]; active=meta[1]>0
    last=(qb*width)//CH
    pair=2*width
    @pl.when(jnp.logical_not(active))
    def _():
        joined_ref[...]=jnp.zeros(joined_ref.shape,bf16)
    @pl.when(active)
    def _():
        qt=q_ref[...].astype(f32).T
        scaled_queries_t(qt, premix, qst, heads, width, size, 0.125, False)
        mx[...]=jnp.full(mx.shape,-1e30,f32)
        def scores(c,diag):
            kc=k_ref[pl.ds(c*CH,CH),:]
            for t in range(heads//2):
                sl=slice(t*pair,(t+1)*pair)
                s=dot(kc,qst[:,sl])
                if diag: s=masked(s,c,qb,width,-1e30)
                s_ref[pl.ds(c*CH,CH),sl]=s
                m=jnp.max(s.reshape(CH//8,8,pair),axis=0)
                mx[:,sl]=jnp.maximum(mx[:,sl],m)
        def body(c,_):
            scores(c,False); return 0
        lax.fori_loop(0,last,body,0)
        scores(last,True)
        peak=jnp.max(mx[...],axis=0,keepdims=True)
        acc[...]=jnp.zeros(acc.shape,f32)
        mx[...]=jnp.zeros(mx.shape,f32)
        def pv(c,_):
            vc=v_ref[pl.ds(c*CH,CH),:]
            for t in range(heads//2):
                sl=slice(t*pair,(t+1)*pair)
                p=jnp.exp(s_ref[pl.ds(c*CH,CH),sl]-peak[:,sl])
                mx[:,sl]+=jnp.sum(p.reshape(CH//8,8,pair),axis=0)
                acc[:,sl]+=dot(vc,p.astype(bf16),0,0)
            return 0
        lax.fori_loop(0,last+1,pv,0)
        total=jnp.sum(mx[...],axis=0,keepdims=True)
        lse_ref[...]=peak+jnp.log(total)
        inv=1.0/total
        for k in range(heads):
            rows=slice(k*size,(k+1)*size)
            out=jnp.zeros((size,width),f32)
            for h in range(heads):
                u=acc[rows,h*width:(h+1)*width]*inv[:,h*width:(h+1)*width]
                ut_ref[rows,h*width:(h+1)*width]=u.astype(bf16)
                out+=u*postmix[h,k]
            acc[rows,0:width]=out
        joined_ref[...]=acc[:,0:width].T.astype(bf16)

VM=60*1024*1024
def att_fwd(meta,premix,postmix,q,k,v):
    width,model=q.shape; seq=k.shape[0]; hw=HEADS*width
    smem=pl.BlockSpec(memory_space=pltpu.SMEM); vmem=pl.BlockSpec(memory_space=pltpu.VMEM)
    return pl.pallas_call(fwd_kernel,
        out_shape=(jax.ShapeDtypeStruct((width,model),bf16),jax.ShapeDtypeStruct((model,hw),bf16),jax.ShapeDtypeStruct((1,hw),f32)),
        in_specs=[smem]*3+[vmem]*3,out_specs=[vmem]*3,
        scratch_shapes=[pltpu.VMEM((model,hw),bf16),pltpu.VMEM((seq,hw),f32),pltpu.VMEM((model,hw),f32),pltpu.VMEM((8,hw),f32)],
        compiler_params=pltpu.CompilerParams(vmem_limit_bytes=VM),
        name="attend_forward",
    )(meta,premix,postmix,q,k,v)

def bwd_kernel(meta,premix,postmix,prerow,postrow,q_ref,up_ref,k_ref,v_ref,ut_ref,lse_ref,
               dq_ref,dk_ref,dv_ref,gpre_ref,gpost_ref,qst,qs,ust,us,acc,pbuf,lbuf,dots):
    width,model=q_ref.shape
    heads=HEADS; size=model//heads
    qb=meta[0]; active=meta[1]>0
    last=(qb*width)//CH
    pair=2*width
    @pl.when(jnp.logical_not(active))
    def _():
        dq_ref[...]=jnp.zeros(dq_ref.shape,bf16)
        gpre_ref[...]=jnp.zeros(gpre_ref.shape,f32)
        gpost_ref[...]=jnp.zeros(gpost_ref.shape,f32)
        dk_ref[...]=jnp.zeros(dk_ref.shape,bf16)
        dv_ref[...]=jnp.zeros(dv_ref.shape,bf16)
    @pl.when(active)
    def _():
        def clear(c,_):
            dk_ref[pl.ds(c*CH,CH),:]=jnp.zeros((CH,model),bf16)
            dv_ref[pl.ds(c*CH,CH),:]=jnp.zeros((CH,model),bf16)
            return 0
        lax.fori_loop(last+1,k_ref.shape[0]//CH,clear,0)
        q=q_ref[...].astype(f32); up=up_ref[...].astype(f32)
        qt=q.T; upt=up.T
        scaled_queries_t(qt, premix, qst, heads, width, size, 0.125, False)
        scaled_queries_t(upt, postmix, ust, heads, width, size, 1.0, True)
        for h in range(heads):
            qs[h*width:(h+1)*width,:]=(q*(prerow[h:h+1,:]*0.125)).astype(bf16)
            us[h*width:(h+1)*width,:]=(up*postrow[h:h+1,:]).astype(bf16)
            ul=ut_ref[:,h*width:(h+1)*width].astype(f32)
            t=jnp.sum((ul*upt).reshape(heads,size,width),axis=1)
            gpost_ref[h]=t
            d=jnp.zeros((1,width),f32)
            for k in range(heads): d+=t[k:k+1,:]*postmix[h,k]
            dots[:,h*width:(h+1)*width]=d
        acc[...]=jnp.zeros(acc.shape,f32)
        def chunk(c,diag):
            kc=k_ref[pl.ds(c*CH,CH),:]
            vc=v_ref[pl.ds(c*CH,CH),:]
            for t in range(heads//2):
                sl=slice(t*pair,(t+1)*pair)
                s=dot(kc,qst[:,sl])
                p=jnp.exp(s-lse_ref[:,sl])
                if diag: p=masked(p,c,qb,width,0.0)
                dp=dot(vc,ust[:,sl])
                l=(p*(dp-dots[:,sl])).astype(bf16)
                pbuf[:,sl]=p.astype(bf16)
                lbuf[:,sl]=l
                acc[:,sl]+=dot(kc,l,0,0)
            dv_ref[pl.ds(c*CH,CH),:]=dot(pbuf[...],us[...]).astype(bf16)
            dk_ref[pl.ds(c*CH,CH),:]=dot(lbuf[...],qs[...]).astype(bf16)
        def body(c,_):
            chunk(c,False); return 0
        lax.fori_loop(0,last,body,0)
        chunk(last,True)
        for g in range(heads):
            rows=slice(g*size,(g+1)*size)
            out=jnp.zeros((size,width),f32)
            qg=qt[rows,:]*0.125
            for h in range(heads):
                a=acc[rows,h*width:(h+1)*width]
                out+=a*premix[g,h]
                gpre_ref[g,h:h+1,:]=jnp.sum(a*qg,axis=0,keepdims=True)
            acc[rows,0:width]=out*0.125
        dq_ref[...]=acc[:,0:width].T.astype(bf16)

def att_bwd(meta,premix,postmix,q,up,k,v,ut,lse):
    width,model=q.shape; seq=k.shape[0]; hw=HEADS*width; size=model//HEADS
    prerow=jnp.repeat(premix.T,size,axis=1); postrow=jnp.repeat(postmix,size,axis=1)
    smem=pl.BlockSpec(memory_space=pltpu.SMEM); vmem=pl.BlockSpec(memory_space=pltpu.VMEM)
    S=jax.ShapeDtypeStruct
    return pl.pallas_call(bwd_kernel,
        out_shape=(S((width,model),bf16),S((seq,model),bf16),S((seq,model),bf16),S((HEADS,HEADS,width),f32),S((HEADS,HEADS,width),f32)),
        in_specs=[smem]*3+[vmem]*8,out_specs=[vmem]*5,
        scratch_shapes=[pltpu.VMEM((model,hw),bf16),pltpu.VMEM((hw,model),bf16),pltpu.VMEM((model,hw),bf16),pltpu.VMEM((hw,model),bf16),
            pltpu.VMEM((model,hw),f32),pltpu.VMEM((CH,hw),bf16),pltpu.VMEM((CH,hw),bf16),pltpu.VMEM((1,hw),f32)],
        compiler_params=pltpu.CompilerParams(vmem_limit_bytes=VM),
        name="attend_backward",
    )(meta,premix,postmix,prerow,postrow,q,up,k,v,ut,lse)


def swap(value, axis, mask):
    count = lax.axis_size(axis)
    return lax.ppermute(value, axis, [(i, i ^ mask) for i in range(count)])


def gather_cores(value, step=2):
    count = lax.axis_size("blk")
    pieces = {}
    for k in range(0, count, 2):
        pieces[k] = value if k == 0 else swap(value, "blk", k)
        pieces[k + 1] = swap(pieces[k], "blk", 1)
    return [pieces[k] for k in range(count)]


def place_rows(pieces, index, axis=0):
    size = pieces[0].shape[axis]
    shape = list(pieces[0].shape)
    shape[axis] = size * len(pieces)
    out = jnp.zeros(shape, pieces[0].dtype)
    for k, piece in enumerate(pieces):
        out = lax.dynamic_update_slice_in_dim(out, piece, (index ^ k) * size, axis)
    return out


def cut(value, index, count, axis=0):
    size = value.shape[axis] // count
    return lax.dynamic_slice_in_dim(value, index * size, size, axis)


def gather_dp(value, zplace):
    count = lax.axis_size("dp")
    return place_rows([value] + [swap(value, "dp", k) for k in range(1, count)], zplace)


def gather_all(value, place, zplace):
    return place_rows(gather_cores(gather_dp(value, zplace)), place)


def scatter_blk(value, place, axis=0):
    count = lax.axis_size("blk")
    keep = [cut(value, place ^ k, count, axis) for k in range(0, count, 2)]
    give = [cut(value, place ^ k ^ 1, count, axis) for k in range(0, count, 2)]
    got = [swap(g.astype(bf16), "blk", 1) for g in give]
    pair = [a.astype(f32) + b.astype(f32) for a, b in zip(keep, got)]
    total = pair[0]
    for i in range(1, count // 2):
        total = total + swap(pair[i].astype(bf16), "blk", 2 * i).astype(f32)
    return total


def scatter_dp(value, zplace):
    count = lax.axis_size("dp")
    total = cut(value, zplace, count)
    for k in range(1, count):
        total = total + swap(cut(value, zplace ^ k, count).astype(bf16), "dp", k).astype(f32)
    return total


def scatter_all(value, place, zplace):
    return scatter_dp(scatter_blk(value, place), zplace)


def gather_group(value):
    one, two = swap(value, "blk", 1), swap(value, "blk", 2)
    return jnp.concatenate([value, one, two, swap(two, "blk", 1)], axis=0)


def scatter_group(value):
    parts = [part.astype(bf16) for part in jnp.split(value, GROUP, axis=0)]
    own = parts[0].astype(f32) + swap(parts[1], "blk", 1).astype(f32)
    across = parts[2].astype(f32) + swap(parts[3], "blk", 1).astype(f32)
    return own + swap(across.astype(bf16), "blk", 2).astype(f32)


def sum_small(value):
    for axis in ("blk", "dp"):
        k = 1
        while k < lax.axis_size(axis):
            value = value + swap(value, axis, k)
            k *= 2
    return value


def inverse_rms(values):
    return lax.rsqrt(jnp.mean(values * values, axis=-1, keepdims=True) + EPSILON)


def norm_back(values, inverse, gain, grad):
    scaled = grad * gain
    back = inverse * (scaled - values * (inverse * inverse * jnp.mean(scaled * values, axis=-1, keepdims=True)))
    return back, jnp.sum(grad * values * inverse, axis=tuple(range(values.ndim - 1)))


def mm(a, b, ca, cb):
    return lax.dot_general(a, b, (((ca,), (cb,)), ((), ())), preferred_element_type=f32)


def on_device(
    inputs, lengths, prenorm, midnorm, query_proj, key_proj, value_proj, output_proj,
    premix, postmix, inner_proj, outer_proj, cotangent,
):
    count, depth = lax.axis_size("blk"), lax.axis_size("dp")
    place, zplace = lax.axis_index("blk"), lax.axis_index("dp")
    rows, width, model = inputs.shape
    mirror = [(i, count - 1 - i) for i in range(count)]
    blocks = [place, count - 1 - place]

    gains = jnp.stack([prenorm, midnorm], axis=1)
    gains = gather_all(gains, place, zplace).astype(f32)
    gain_first, gain_second = gains[:, 0], gains[:, 1]
    x_all = place_rows(gather_cores(inputs), place, axis=1)
    wqkv = gather_all(jnp.concatenate([query_proj, key_proj, value_proj], axis=1), place, zplace)
    output_w = gather_all(output_proj, place, zplace)
    query_w, key_w, value_w = wqkv[:, :model], wqkv[:, model:2 * model], wqkv[:, 2 * model:]

    bands = count // GROUP
    band_ff = depth * outer_proj.shape[0]
    outer_rows = gather_dp(outer_proj, zplace)
    outer_w = place_rows(
        [outer_rows] + [swap(outer_rows, "blk", GROUP * j) for j in range(1, bands)], place // GROUP
    )
    inner_rows = gather_dp(inner_proj, zplace)
    wide = inner_rows.reshape(inner_rows.shape[0], bands, GROUP, band_ff)
    inner_parts = []
    for k in range(count):
        part = lax.dynamic_index_in_dim(wide, (place ^ k) % GROUP, 2, keepdims=False)
        part = part.reshape(part.shape[0], bands * band_ff)
        inner_parts.append(part if k == 0 else swap(part, "blk", k))
    inner_w = place_rows(inner_parts, place)

    cot = jnp.stack([cotangent[0], lax.ppermute(cotangent[1], "blk", mirror)])
    offsets = jnp.arange(width, dtype=jnp.int32)
    valid = jnp.stack([(blocks[r] * width + offsets < lengths[r]) for r in range(rows)]).astype(f32)[..., None]
    upgrad = cot.astype(f32) * valid
    up_all = gather_group(upgrad.astype(bf16).reshape(rows * width, model))

    residual_all = x_all.astype(f32)
    inverse_all = inverse_rms(residual_all)
    normed_all = (residual_all * inverse_all * gain_first).astype(bf16)

    def own(value):
        return jnp.stack([lax.dynamic_slice_in_dim(value[r], blocks[r] * width, width, 0) for r in range(rows)])

    keys = mm(normed_all, key_w, 2, 0).astype(bf16)
    values = mm(normed_all, value_w, 2, 0).astype(bf16)
    normed_own = own(normed_all)
    residual = own(residual_all)
    queries = mm(normed_own, query_w, 2, 0).astype(bf16)
    metas = [
        jnp.stack([blocks[r], (blocks[r] * width < lengths[r]).astype(jnp.int32)]) for r in range(rows)
    ]
    forward = [att_fwd(metas[r], premix, postmix, queries[r], keys[r], values[r]) for r in range(rows)]
    joined = jnp.stack([f[0] for f in forward])
    middle = residual + mm(joined, output_w, 2, 0)
    inverse_mid = inverse_rms(middle)
    second = (middle * inverse_mid * gain_second).astype(bf16)
    second_all = gather_group(second.reshape(rows * width, model))
    inner = mm(second_all, inner_w, 1, 0)
    activated, act_back = jax.vjp(lambda v: jax.nn.gelu(v, approximate=True), inner)
    hidden = activated.astype(bf16)
    outer = scatter_group(mm(hidden, outer_w, 1, 0)).reshape(rows, width, model)
    result = (valid * (middle + outer)).astype(bf16)
    outputs = jnp.stack([result[0], lax.ppermute(result[1], "blk", mirror)])
    hidden_grad = mm(up_all, outer_w, 1, 1)
    inner_cast = act_back(hidden_grad)[0].astype(bf16)
    second_grad = scatter_group(mm(inner_cast, inner_w, 1, 1)).reshape(rows, width, model)
    outer_wgrad = mm(hidden, up_all, 0, 0)
    inner_wgrad = mm(second_all, inner_cast, 0, 0)
    middle_part, gain_second_grad = norm_back(middle, inverse_mid, gain_second, second_grad)
    middle_grad = upgrad + middle_part
    middle_cast = middle_grad.astype(bf16)
    flat = rows * width
    output_wgrad = mm(joined.reshape(flat, model), middle_cast.reshape(flat, model), 0, 0)
    upstream = mm(middle_cast, output_w, 2, 1).astype(bf16)

    back = [
        att_bwd(metas[r], premix, postmix, queries[r], upstream[r], keys[r], values[r], forward[r][1], forward[r][2])
        for r in range(rows)
    ]
    query_cast = jnp.stack([b[0] for b in back])
    key_cast = jnp.stack([b[1] for b in back])
    value_cast = jnp.stack([b[2] for b in back])
    pre_grad = jnp.sum(back[0][3] + back[1][3], axis=-1)
    post_grad = jnp.sum(back[0][4] + back[1][4], axis=-1)
    length = keys.shape[1]
    normed_flat = normed_all.reshape(rows * length, model)
    query_wgrad = mm(normed_own.reshape(flat, model), query_cast.reshape(flat, model), 0, 0)
    key_wgrad = mm(normed_flat, key_cast.reshape(rows * length, model), 0, 0)
    value_wgrad = mm(normed_flat, value_cast.reshape(rows * length, model), 0, 0)
    normed_grad = mm(key_cast, key_w, 2, 1) + mm(value_cast, value_w, 2, 1)
    query_part = mm(query_cast, query_w, 2, 1)

    def put(base, part):
        return jnp.stack([
            lax.dynamic_update_slice_in_dim(
                base[r],
                lax.dynamic_slice_in_dim(base[r], blocks[r] * width, width, 0) + part[r],
                blocks[r] * width, 0,
            )
            for r in range(rows)
        ])

    normed_grad = put(normed_grad, query_part)
    input_part, gain_first_grad = norm_back(residual_all, inverse_all, gain_first, normed_grad)
    input_part = put(input_part, middle_grad)
    grad_inputs = scatter_blk(input_part, place, axis=1).astype(bf16)

    output_sum = scatter_all(output_wgrad, place, zplace)
    qkv_sum = scatter_all(jnp.concatenate([query_wgrad, key_wgrad, value_wgrad], axis=1), place, zplace)
    outer_sum = cut(outer_wgrad, place // GROUP, bands)
    for j in range(1, bands):
        outer_sum = outer_sum + swap(
            cut(outer_wgrad, (place // GROUP) ^ j, bands).astype(bf16), "blk", GROUP * j
        ).astype(f32)
    outer_sum = scatter_dp(outer_sum, zplace)
    member = [None] * GROUP
    for k in range(count):
        part = cut(inner_wgrad, place ^ k, count)
        part = part if k == 0 else swap(part.astype(bf16), "blk", k).astype(f32)
        member[k % GROUP] = part if member[k % GROUP] is None else member[k % GROUP] + part
    inner_sum = jnp.zeros((model // count, bands, GROUP, band_ff), f32)
    for i in range(GROUP):
        inner_sum = lax.dynamic_update_slice_in_dim(
            inner_sum, member[i].reshape(model // count, bands, 1, band_ff), (place % GROUP) ^ i, 2
        )
    inner_sum = scatter_dp(inner_sum.reshape(model // count, inner_proj.shape[1]), zplace)

    small = jnp.concatenate([gain_first_grad, gain_second_grad, pre_grad.reshape(-1), post_grad.reshape(-1)])
    small = sum_small(jnp.pad(small, (0, -small.shape[0] % 1024)).reshape(-1, 128)).reshape(-1)
    shard = prenorm.shape[0]
    start = (place * depth + zplace) * shard
    heads = premix.shape[0]
    mixes = small[2 * model:2 * model + 2 * heads * heads].reshape(2, heads, heads)
    return (
        outputs,
        grad_inputs,
        lax.dynamic_slice_in_dim(small, start, shard, 0),
        lax.dynamic_slice_in_dim(small, model + start, shard, 0),
        qkv_sum[:, :model],
        qkv_sum[:, model:2 * model],
        qkv_sum[:, 2 * model:],
        output_sum,
        mixes[0],
        mixes[1],
        inner_sum,
        outer_sum,
    )


def solution(mesh):
    weight = P(("blk", "dp"), None)
    vector = P(("blk", "dp"))
    tokens = P("dp", "blk", None)
    in_specs = (
        tokens, P("dp"), vector, vector, weight, weight, weight, weight, P(), P(), weight, weight, tokens,
    )
    out_specs = (
        tokens, tokens, vector, vector, weight, weight, weight, weight, P(), P(), weight, weight,
    )
    return jax.shard_map(on_device, mesh=mesh, in_specs=in_specs, out_specs=out_specs, check_vma=False)
```

time: 1510 us -> 545 us (0.36)
  waiting for transfers between devices: 734 us -> 132 us
  starting transfers between devices: 435 us -> 103 us
  local copies, waits for them, and re-layouts: 48.4 us -> 143 us
  blocking collectives: 82.2 us -> 0 us
  matrix products: 120 us -> 58.3 us
  Pallas kernels: 0 us -> 58.7 us
  other arithmetic: 55 us -> 38.4 us
    reduce_scatter x6 -> x0, waiting for transfers between devices: 522 us -> none  [the longest x1 142 us: on_device(): lax.psum_scatter(ffn_totals[1], ('blk', 'dp'), scatter_dimension=0, tiled...]
    ppermute x65 -> x111, starting transfers between devices: 434 us -> 103 us  [the longest x109 102 us: swap(): return lax.ppermute(value, axis, [(i, i ^ mask) for i in range(count)])]
    all_gather x6 -> x0, waiting for transfers between devices: 106 us -> none  [the longest x1 53.8 us: on_device(): lax.all_gather(query_proj, ('blk', 'dp'), axis=0, tiled=True)]
    unnamed x2 -> x0, blocking collectives: 82.2 us -> none
    dynamic_update_slice x0 -> x66, local copies, waits for them, and re-layouts: none -> 71.8 us  [the longest x62 43.8 us: place_rows(): out = lax.dynamic_update_slice_in_dim(out, piece, (index ^ k) * size, axis)]
    dot_general x45 -> x18, matrix products: 120 us -> 58.3 us  [mm(): lax.dot_general(a, b, (((ca,), (cb,)), ((), ())), preferred_element_type=...]
    pallas_call x0 -> x4, Pallas kernels: none -> 58.7 us  [the longest x2 39.9 us: att_bwd(): pl.pallas_call(bwd_kernel, out_shape=(S((width, model), bf16), S((seq, mo...]
    ppermute x65 -> x111, waiting for transfers between devices: 100 us -> 132 us  [the longest x109 122 us: swap(): return lax.ppermute(value, axis, [(i, i ^ mask) for i in range(count)])]
  transfers between devices with their start and end apart: 77 -> 111, of which waited for: 34 -> 35; matrix products, arithmetic and copies ran while one was open for 11% -> 38% of each run, Pallas kernels for 0% -> 3%
where the time goes in v1:
time: 545 us; the launch traced here: 537 us
  local copies, waits for them, and re-layouts  143 us (26%)
  waiting for transfers between devices  132 us (24%)
  starting transfers between devices  103 us (19%)
  Pallas kernels  58.7 us (11%)
  matrix products  58.3 us (11%)
  other arithmetic  38.4 us (7%)
    ppermute x109, waiting for transfers between devices, swap(): return lax.ppermute(value, axis, [(i, i ^ mask) for i in range(count)])  122 us
    ppermute x109, starting transfers between devices, swap(): return lax.ppermute(value, axis, [(i, i ^ mask) for i in range(count)])  102 us
    dot_general x18, matrix products, mm(): lax.dot_general(a, b, (((ca,), (cb,)), ((), ())), preferred_element_type=...  58.3 us
    dynamic_update_slice x62, local copies, waits for them, and re-layouts, place_rows(): out = lax.dynamic_update_slice_in_dim(out, piece, (index ^ k) * size, axis)  43.8 us
    pallas_call x2, Pallas kernels, att_bwd(): pl.pallas_call(bwd_kernel, out_shape=(S((width, model), bf16), S((seq, mo...  39.9 us
    dynamic_update_slice x4, local copies, waits for them, and re-layouts, on_device(): lax.dynamic_update_slice_in_dim(inner_sum, member[i].reshape(model // cou...  28 us
    pallas_call x2, Pallas kernels, att_fwd(): pl.pallas_call(fwd_kernel, out_shape=(jax.ShapeDtypeStruct((width, model)...  18.8 us
    unnamed x138, local copies, waits for them, and re-layouts  12.2 us
  transfers between devices with their start and end apart: 111, of which 35 were waited for; matrix products, arithmetic and copies ran while one was open for 38% of the time, Pallas kernels for 3%

profile of v1, /device:TPU:0, one launch (start us, length us, event | category | flops | bytes accessed | tf_op | source)
XLA Modules:
  0.0 537.4 jit_solution(15635428081293302754)
XLA Ops:
  1.4 3.1 collective-permute-start.7
  48.2 2.9 collective-permute-start.28
  53.3 4.0 collective-permute-start.29
  63.7 3.1 collective-permute-start.19
  78.5 3.5 collective-permute-start.42
  90.9 10.9 %dynamic-slice_reduce_fusion = (bf16[96,2,384]{2,1,0:T(2,128)(2,1)S(1)}, bf16[96,2,384]{2,1,0:T(2,128)(2,1)S(1)}, bf16[96,2,384]{2,1,0:T(2,128)(2,1)S(1)}, bf16[...) fusion(bf16[96,2,4,384]{3,2,1,0:T(4,128)(2,1)} %reshape.232, ...), kind=kLoop, calls=%fused_computation.155 | loop fusion | bytes 2359328 | tf_op jit(solution)/shard_map/jit(dynamic_index_in_dim)/dynamic_slice | solution.py:299
  101.9 3.9 collective-permute-start.52
  119.9 4.4 collective-permute-done.58
  124.5 2.8 collective-permute-done.33
  130.3 4.0 collective-permute-done.35
  145.0 13.6 %collective-permute-done.21 = bf16[96,2304]{1,0:T(8,128)(2,1)S(1)} collective-permute-done((bf16[96,2304]{1,0:T(8,128)(2,1)}, bf16[96,2304]{1,0:T(8,128)(2,1)S(1)}, u32[]{:S(2)}, u32[]{:S(2)}) %collective-permute-start.21) | collective-permute-done | bytes 442400 | tf_op jit(solution)/shard_map/ppermute | solution.py:176
  173.6 4.1 convolution_convert_fusion.1
  177.7 4.1 convolution_convert_fusion
  187.1 6.8 %attend_forward.2 = (bf16[128,768]{1,0:T(8,128)(2,1)}, bf16[768,1536]{1,0:T(8,128)(2,1)}, f32[1,1536]{1,0:T(1,128)}) custom-call(s32[2]{0:T(128)} %get-tuple-element.187.meta, f32[12,12]{1,0:T(8,128)} %premix.7, f32[12,12]{1,0:T(8,128)} %postmix.7, bf16[128,768]{1,0:T(8,128)(2,1)} %get-tuple-element.171.q_ref, bf16[1024,768]{1,0:T(8,128)(2,1)} %get-tuple-element.192.k_ref, ...), custom_call_target="tpu_custom_call" | custom-call | tf_op jit(solution)/shard_map/attend_forward/pallas_call | solution.py:86
  193.9 12.0 %attend_forward.3 = (bf16[128,768]{1,0:T(8,128)(2,1)}, bf16[768,1536]{1,0:T(8,128)(2,1)}, f32[1,1536]{1,0:T(1,128)}) custom-call(s32[2]{0:T(128)} %get-tuple-element.188.meta, f32[12,12]{1,0:T(8,128)} %premix.7, f32[12,12]{1,0:T(8,128)} %postmix.7, bf16[128,768]{1,0:T(8,128)(2,1)} %get-tuple-element.172.q_ref, bf16[1024,768]{1,0:T(8,128)(2,1)} %get-tuple-element.191.k_ref, ...), custom_call_target="tpu_custom_call" | custom-call | tf_op jit(solution)/shard_map/attend_forward/pallas_call | solution.py:86
  216.8 3.5 collective-permute-done.47
  223.3 10.1 %collective-permute-done.49 = bf16[96,768]{1,0:T(8,128)(2,1)S(1)} collective-permute-done((bf16[96,768]{1,0:T(8,128)(2,1)S(1)}, bf16[96,768]{1,0:T(8,128)(2,1)S(1)}, u32[]{:S(2)}, u32[]{:S(2)}) %collective-permute-start.49) | collective-permute-done | bytes 147488 | tf_op jit(solution)/shard_map/ppermute | solution.py:176
  239.9 2.7 collective-permute-start.107
  244.6 4.6 fusion.14
  256.3 2.7 collective-permute-start.101
  282.0 7.0 %dynamic_update_slice.280 = f32[96,2,4,384]{3,2,1,0:T(4,128)} dynamic-update-slice(f32[96,2,4,384]{3,2,1,0:T(4,128)} %broadcast_in_dim.50, f32[96,2,1,384]{3,2,1,0:T(1,128)} %reshape.266, s32[]{:T(128)} %constant.142.clone.1, s32[]{:T(128)} %constant.142.clone.1, s32[]{:T(128)S(6)} %select_n.302, s32[]{:T(128)} %constant.142.clone.1) | dynamic-update-slice | bytes 589828 | tf_op jit(solution)/shard_map/dynamic_update_slice | solution.py:396
  289.0 7.0 %dynamic_update_slice.281 = f32[96,2,4,384]{3,2,1,0:T(4,128)} dynamic-update-slice(f32[96,2,4,384]{3,2,1,0:T(4,128)} %dynamic_update_slice.280, f32[96,2,1,384]{3,2,1,0:T(1,128)} %reshape.267, s32[]{:T(128)} %constant.142.clone.1, s32[]{:T(128)} %constant.142.clone.1, s32[]{:T(128)S(6)} %select_n.332, s32[]{:T(128)} %constant.142.clone.1) | dynamic-update-slice | bytes 589828 | tf_op jit(solution)/shard_map/dynamic_update_slice | solution.py:396
  296.0 7.0 %dynamic_update_slice.282 = f32[96,2,4,384]{3,2,1,0:T(4,128)} dynamic-update-slice(f32[96,2,4,384]{3,2,1,0:T(4,128)} %dynamic_update_slice.281, f32[96,2,1,384]{3,2,1,0:T(1,128)} %reshape.268, s32[]{:T(128)} %constant.142.clone.1, s32[]{:T(128)} %constant.142.clone.1, s32[]{:T(128)S(6)} %select_n.333, s32[]{:T(128)} %constant.142.clone.1) | dynamic-update-slice | bytes 589828 | tf_op jit(solution)/shard_map/dynamic_update_slice | solution.py:396
  303.0 7.0 %dynamic_update_slice.283 = f32[96,2,4,384]{3,2,1,0:T(4,128)} dynamic-update-slice(f32[96,2,4,384]{3,2,1,0:T(4,128)} %dynamic_update_slice.282, f32[96,2,1,384]{3,2,1,0:T(1,128)} %reshape.269, s32[]{:T(128)} %constant.142.clone.1, s32[]{:T(128)} %constant.142.clone.1, s32[]{:T(128)S(6)} %select_n.334, s32[]{:T(128)} %constant.142.clone.1) | dynamic-update-slice | bytes 589828 | tf_op jit(solution)/shard_map/dynamic_update_slice | solution.py:396
  310.0 2.9 reshape.253
  321.8 8.5 %collective-permute-done.105 = bf16[24,3072]{1,0:T(8,128)(2,1)S(1)} collective-permute-done((bf16[24,3072]{1,0:T(8,128)(2,1)S(1)}, bf16[24,3072]{1,0:T(8,128)(2,1)S(1)}, u32[]{:S(2)}, u32[]{:S(2)}) %collective-permute-start.105) | collective-permute-done | bytes 147488 | tf_op jit(solution)/shard_map/ppermute | solution.py:176
  334.3 3.6 collective-permute-start.108
  342.4 8.6 %collective-permute-done.109 = bf16[96,768]{1,0:T(8,128)(2,1)S(1)} collective-permute-done((bf16[96,768]{1,0:T(8,128)(2,1)S(1)}, bf16[96,768]{1,0:T(8,128)(2,1)S(1)}, u32[]{:S(2)}, u32[]{:S(2)}) %collective-permute-start.109) | collective-permute-done | bytes 147488 | tf_op jit(solution)/shard_map/ppermute | solution.py:176
  353.8 6.6 %collective-permute-done.56 = bf16[256,768]{1,0:T(8,128)(2,1)S(1)} collective-permute-done((bf16[256,768]{1,0:T(8,128)(2,1)S(1)}, bf16[256,768]{1,0:T(8,128)(2,1)S(1)}, u32[]{:S(2)}, u32[]{:S(2)}) %collective-permute-start.56) | collective-permute-done | bytes 393248 | tf_op jit(solution)/shard_map/ppermute | solution.py:176
  366.1 13.1 %attend_backward.2 = (bf16[128,768]{1,0:T(8,128)(2,1)}, bf16[1024,768]{1,0:T(8,128)(2,1)}, bf16[1024,768]{1,0:T(8,128)(2,1)}, f32[12,12,128]{2,1,0:T(8,128)}, f32[12,12,128]{2,1,0:T(8,128)}) custom-call(s32[2]{0:T(128)} %get-tuple-element.187.meta, f32[12,12]{1,0:T(8,128)} %premix.7, f32[12,12]{1,0:T(8,128)} %postmix.7, f32[12,768]{1,0:T(8,128)} %reshape.242.prerow, ...), custom_call_target="tpu_custom_call" | custom-call | tf_op jit(solution)/shard_map/attend_backward/pallas_call | solution.py:164
  379.2 26.8 %attend_backward.3 = (bf16[128,768]{1,0:T(8,128)(2,1)}, bf16[1024,768]{1,0:T(8,128)(2,1)}, bf16[1024,768]{1,0:T(8,128)(2,1)}, f32[12,12,128]{2,1,0:T(8,128)}, f32[12,12,128]{2,1,0:T(8,128)}) custom-call(s32[2]{0:T(128)} %get-tuple-element.188.meta, f32[12,12]{1,0:T(8,128)} %premix.7, f32[12,12]{1,0:T(8,128)} %postmix.7, f32[12,768]{1,0:T(8,128)} %reshape.242.prerow, ...), custom_call_target="tpu_custom_call" | custom-call | tf_op jit(solution)/shard_map/attend_backward/pallas_call | solution.py:164
  406.0 3.0 convolution_bitcast_fusion.1
  409.0 2.8 fusion.22
  411.8 5.7 %fusion.19 = f32[768,768]{1,0:T(8,128)} fusion(bf16[2,1024,768]{2,1,0:T(8,128)(2,1)S(1)} %copy-done.6, bf16[1,1024,768]{2,1,0:T(8,128)(2,1)} %bitcast.147, bf16[1,1024,768]{2,1,0:T(8,128)(2,1)S(1)} %bitcast.145), kind=kOutput, calls=%fused_computation.50 | convolution fusion | flops 2417491968 | bytes 8650752 | tf_op jit(solution)/shard_map/dot_general | solution.py:268
  417.5 6.0 %fusion.16 = f32[2,1024,768]{2,1,0:T(8,128)} fusion(bf16[1,1024,768]{2,1,0:T(8,128)(2,1)S(1)} %bitcast.148, bf16[1,1024,768]{2,1,0:T(8,128)(2,1)S(1)} %bitcast.146, bf16[768,2304]{1,0:T(8,128)(2,1)} %constant_dynamic-update-slice_fusion.30), kind=kOutput, calls=%fused_computation.47 | convolution fusion | flops 2417491968 | bytes 10616832 | tf_op jit(solution)/shard_map/dot_general | solution.py:268
  428.3 7.1 %fusion.18 = f32[768,768]{1,0:T(8,128)} fusion(bf16[2,1024,768]{2,1,0:T(8,128)(2,1)} %copy-done.5, bf16[1,1024,768]{2,1,0:T(8,128)(2,1)} %bitcast.143, bf16[1,1024,768]{2,1,0:T(8,128)(2,1)} %bitcast.141), kind=kOutput, calls=%fused_computation.49 | convolution fusion | flops 2417491968 | bytes 8650752 | tf_op jit(solution)/shard_map/dot_general | solution.py:268
  435.4 4.0 convolution_add_fusion
  443.5 3.6 fusion.5
  453.6 3.5 collective-permute-done.74
  457.1 3.6 collective-permute-done.75
  462.0 3.3 collective-permute-done.76
  468.2 2.7 collective-permute-start.93
  474.4 3.3 collective-permute-done.91
  479.5 5.6 %collective-permute-done.57 = bf16[128,768]{1,0:T(8,128)(2,1)S(1)} collective-permute-done((bf16[128,768]{1,0:T(8,128)(2,1)S(1)}, bf16[128,768]{1,0:T(8,128)(2,1)S(1)}, u32[]{:S(2)}, u32[]{:S(2)}) %collective-permute-start.57) | collective-permute-done | bytes 196640 | tf_op jit(solution)/shard_map/ppermute | solution.py:336
  485.9 3.2 collective-permute-done.94
  501.5 7.1 %collective-permute-done.79 = bf16[96,2304]{1,0:T(8,128)(2,1)S(1)} collective-permute-done((bf16[96,2304]{1,0:T(8,128)(2,1)S(1)}, bf16[96,2304]{1,0:T(8,128)(2,1)S(1)}, u32[]{:S(2)}, u32[]{:S(2)}) %collective-permute-start.79) | collective-permute-done | bytes 442400 | tf_op jit(solution)/shard_map/ppermute | solution.py:176
  510.0 8.6 %collective-permute-done.81 = bf16[96,2304]{1,0:T(8,128)(2,1)S(1)} collective-permute-done((bf16[96,2304]{1,0:T(8,128)(2,1)S(1)}, bf16[96,2304]{1,0:T(8,128)(2,1)S(1)}, u32[]{:S(2)}, u32[]{:S(2)}) %collective-permute-start.81) | collective-permute-done | bytes 442400 | tf_op jit(solution)/shard_map/ppermute | solution.py:176
  528.9 6.5 %collective-permute-done.69 = bf16[2,128,768]{2,1,0:T(8,128)(2,1)S(1)} collective-permute-done((bf16[2,128,768]{2,1,0:T(8,128)(2,1)S(1)}, bf16[2,128,768]{2,1,0:T(8,128)(2,1)S(1)}, u32[]{:S(2)}, u32[]{:S(2)}) %collective-permute-start.69) | collective-permute-done | bytes 393248 | tf_op jit(solution)/shard_map/ppermute | solution.py:176
  (508 shorter events, 249.2 us)
Async XLA Ops:
  1.4 27.5 %collective-permute-start.7 = (bf16[24,2]{0,1:T(2,128)(2,1)S(1)}, bf16[24,2]{0,1:T(2,128)(2,1)}, u32[]{:S(2)}, u32[]{:S(2)}) collective-permute-start(bf16[24,2]{0,1:T(2,128)(2,1)S(1)} %pad_maximum_fusion.30), channel_id=1, source_target_pairs={{0,1},{1,0},{2,3},{3,2},{4,5},{5,4},{6,7},{7,6},{8,9},{9,8},{10,11... | collective-permute-start | bytes 296 | tf_op jit(solution)/shard_map/ppermute | solution.py:176
  4.4 25.7 %collective-permute-start.8 = (bf16[24,2]{0,1:T(2,128)(2,1)S(1)}, bf16[24,2]{0,1:T(2,128)(2,1)}, u32[]{:S(2)}, u32[]{:S(2)}) collective-permute-start(bf16[24,2]{0,1:T(2,128)(2,1)S(1)} %pad_maximum_fusion.30), channel_id=1, source_target_pairs={{0,2},{1,3},{2,0},{3,1},{4,6},{5,7},{6,4},{7,5},{8,10},{9,11},{10,... | collective-permute-start | bytes 296 | tf_op jit(solution)/shard_map/ppermute | solution.py:176
  7.0 24.4 %collective-permute-start.9 = (bf16[24,2]{0,1:T(2,128)(2,1)S(1)}, bf16[24,2]{0,1:T(2,128)(2,1)S(1)}, u32[]{:S(2)}, u32[]{:S(2)}) collective-permute-start(bf16[24,2]{0,1:T(2,128)(2,1)S(1)} %pad_maximum_fusion.30), channel_id=1, source_target_pairs={{0,3},{1,2},{2,1},{3,0},{4,7},{5,6},{6,5},{7,4},{8,11},{9,10},{10,... | collective-permute-start | bytes 296 | tf_op jit(solution)/shard_map/ppermute | solution.py:176
  7.0 131.4 %collective-permute-start = (bf16[2,128,768]{2,1,0:T(8,128)(2,1)}, bf16[2,128,768]{2,1,0:T(8,128)(2,1)}, u32[]{:S(2)}, u32[]{:S(2)}) collective-permute-start(bf16[2,128,768]{2,1,0:T(8,128)(2,1)} %param.13), channel_id=1, source_target_pairs={{0,4},{4,0},{8,12},{12,8},{16,20},{20,16},{24,28},{28,24},{1,5},{5... | collective-permute-start | bytes 1179656 | tf_op jit(solution)/shard_map/ppermute | solution.py:176
  37.3 103.5 %collective-permute-start.1 = (bf16[2,128,768]{2,1,0:T(8,128)(2,1)}, bf16[2,128,768]{2,1,0:T(8,128)(2,1)}, u32[]{:S(2)}, u32[]{:S(2)}) collective-permute-start(bf16[2,128,768]{2,1,0:T(8,128)(2,1)} %param.13), channel_id=1, source_target_pairs={{0,8},{4,12},{8,0},{12,4},{16,24},{20,28},{24,16},{28,20},{1,9},{5... | collective-permute-start | bytes 1179656 | tf_op jit(solution)/shard_map/ppermute | solution.py:176
  41.2 102.1 %collective-permute-start.3 = (bf16[2,128,768]{2,1,0:T(8,128)(2,1)}, bf16[2,128,768]{2,1,0:T(8,128)(2,1)}, u32[]{:S(2)}, u32[]{:S(2)}) collective-permute-start(bf16[2,128,768]{2,1,0:T(8,128)(2,1)} %param.13), channel_id=1, source_target_pairs={{0,16},{4,20},{8,24},{12,28},{16,0},{20,4},{24,8},{28,12},{1,17},{... | collective-permute-start | bytes 1179656 | tf_op jit(solution)/shard_map/ppermute | solution.py:176
  42.2 21.6 %collective-permute-start.17 = (bf16[24,2304]{1,0:T(8,128)(2,1)S(1)}, bf16[24,2304]{1,0:T(8,128)(2,1)}, u32[]{:S(2)}, u32[]{:S(2)}) collective-permute-start(bf16[24,2304]{1,0:T(8,128)(2,1)S(1)} %constant_dynamic-update-slice_fusion.50), channel_id=1, source_target_pairs={{0,1},{1,0},{2,3},{3,2},{4,5},{5,4},{6,7},{7,6},{8,9},{9,8},{10,11... | collective-permute-start | bytes 331784 | tf_op jit(solution)/shard_map/ppermute | solution.py:176
  82.7 19.2 %collective-permute-start.50 = (bf16[96,768]{1,0:T(8,128)(2,1)}, bf16[96,768]{1,0:T(8,128)(2,1)S(1)}, u32[]{:S(2)}, u32[]{:S(2)}) collective-permute-start(bf16[96,768]{1,0:T(8,128)(2,1)} %param.24), channel_id=1, source_target_pairs={{0,1},{1,0},{2,3},{3,2},{4,5},{5,4},{6,7},{7,6},{8,9},{9,8},{10,11... | collective-permute-start | bytes 442376 | tf_op jit(solution)/shard_map/ppermute | solution.py:176
  85.5 20.9 %collective-permute-start.51 = (bf16[96,768]{1,0:T(8,128)(2,1)}, bf16[96,768]{1,0:T(8,128)(2,1)}, u32[]{:S(2)}, u32[]{:S(2)}) collective-permute-start(bf16[96,768]{1,0:T(8,128)(2,1)} %param.24), channel_id=1, source_target_pairs={{0,2},{1,3},{2,0},{3,1},{4,6},{5,7},{6,4},{7,5},{8,10},{9,11},{10,... | collective-permute-start | bytes 442376 | tf_op jit(solution)/shard_map/ppermute | solution.py:176
  136.2 23.2 %collective-permute-start.5 = (bf16[2,128,768]{2,1,0:T(8,128)(2,1)S(1)}, bf16[2,128,768]{2,1,0:T(8,128)(2,1)S(1)}, u32[]{:S(2)}, u32[]{:S(2)}) collective-permute-start(bf16[2,128,768]{2,1,0:T(8,128)(2,1)S(1)} %copy-done.33), channel_id=1, source_target_pairs={{0,24},{4,28},{8,16},{12,20},{16,8},{20,12},{24,0},{28,4},{1,25},{... | collective-permute-start | bytes 1179656 | tf_op jit(solution)/shard_map/ppermute | solution.py:176
  138.5 20.1 %collective-permute-start.21 = (bf16[96,2304]{1,0:T(8,128)(2,1)}, bf16[96,2304]{1,0:T(8,128)(2,1)S(1)}, u32[]{:S(2)}, u32[]{:S(2)}) collective-permute-start(bf16[96,2304]{1,0:T(8,128)(2,1)} %constant_dynamic-update-slice_fusion.38), channel_id=1, source_target_pairs={{0,8},{4,12},{8,0},{12,4},{16,24},{20,28},{24,16},{28,20},{1,9},{5... | collective-permute-start | bytes 1327112 | tf_op jit(solution)/shard_map/ppermute | solution.py:176
  140.8 25.0 %collective-permute-start.23 = (bf16[96,2304]{1,0:T(8,128)(2,1)}, bf16[96,2304]{1,0:T(8,128)(2,1)S(1)}, u32[]{:S(2)}, u32[]{:S(2)}) collective-permute-start(bf16[96,2304]{1,0:T(8,128)(2,1)} %constant_dynamic-update-slice_fusion.38), channel_id=1, source_target_pairs={{0,16},{4,20},{8,24},{12,28},{16,0},{20,4},{24,8},{28,12},{1,17},{... | collective-permute-start | bytes 1327112 | tf_op jit(solution)/shard_map/ppermute | solution.py:176
  142.5 17.4 %collective-permute-start.2 = (bf16[2,128,768]{2,1,0:T(8,128)(2,1)}, bf16[2,128,768]{2,1,0:T(8,128)(2,1)S(1)}, u32[]{:S(2)}, u32[]{:S(2)}) collective-permute-start(bf16[2,128,768]{2,1,0:T(8,128)(2,1)} %collective-permute-done.1), channel_id=1, source_target_pairs={{0,4},{4,0},{8,12},{12,8},{16,20},{20,16},{24,28},{28,24},{1,5},{5... | collective-permute-start | bytes 1179656 | tf_op jit(solution)/shard_map/ppermute | solution.py:176
  143.4 25.6 %collective-permute-start.25 = (bf16[96,2304]{1,0:T(8,128)(2,1)}, bf16[96,2304]{1,0:T(8,128)(2,1)S(1)}, u32[]{:S(2)}, u32[]{:S(2)}) collective-permute-start(bf16[96,2304]{1,0:T(8,128)(2,1)} %constant_dynamic-update-slice_fusion.38), channel_id=1, source_target_pairs={{0,24},{4,28},{8,16},{12,20},{16,8},{20,12},{24,0},{28,4},{1,25},{... | collective-permute-start | bytes 1327112 | tf_op jit(solution)/shard_map/ppermute | solution.py:176
  159.3 74.6 %collective-permute-start.53 = (bf16[384,768]{1,0:T(8,128)(2,1)}, bf16[384,768]{1,0:T(8,128)(2,1)}, u32[]{:S(2)}, u32[]{:S(2)}) collective-permute-start(bf16[384,768]{1,0:T(8,128)(2,1)} %constant_dynamic-update-slice_fusion.2), channel_id=1, source_target_pairs={{0,16},{4,20},{8,24},{12,28},{16,0},{20,4},{24,8},{28,12},{1,17},{... | collective-permute-start | bytes 1769480 | tf_op jit(solution)/shard_map/ppermute | solution.py:176
  161.2 48.1 %collective-permute-start.43 = (bf16[96,768]{1,0:T(8,128)(2,1)}, bf16[96,768]{1,0:T(8,128)(2,1)}, u32[]{:S(2)}, u32[]{:S(2)}) collective-permute-start(bf16[96,768]{1,0:T(8,128)(2,1)} %bitcast.47), channel_id=1, source_target_pairs={{0,4},{4,0},{8,12},{12,8},{16,20},{20,16},{24,28},{28,24},{1,5},{5... | collective-permute-start | bytes 442376 | tf_op jit(solution)/shard_map/ppermute | solution.py:176
  165.8 45.2 %collective-permute-start.44 = (bf16[96,768]{1,0:T(8,128)(2,1)}, bf16[96,768]{1,0:T(8,128)(2,1)}, u32[]{:S(2)}, u32[]{:S(2)}) collective-permute-start(bf16[96,768]{1,0:T(8,128)(2,1)} %bitcast.49), channel_id=1, source_target_pairs={{0,8},{4,12},{8,0},{12,4},{16,24},{20,28},{24,16},{28,20},{1,9},{5... | collective-permute-start | bytes 442376 | tf_op jit(solution)/shard_map/ppermute | solution.py:176
  169.0 43.0 %collective-permute-start.45 = (bf16[96,768]{1,0:T(8,128)(2,1)}, bf16[96,768]{1,0:T(8,128)(2,1)}, u32[]{:S(2)}, u32[]{:S(2)}) collective-permute-start(bf16[96,768]{1,0:T(8,128)(2,1)} %bitcast.51), channel_id=1, source_target_pairs={{0,12},{4,8},{8,4},{12,0},{16,28},{20,24},{24,20},{28,16},{1,13},{... | collective-permute-start | bytes 442376 | tf_op jit(solution)/shard_map/ppermute | solution.py:176
  171.3 43.9 %collective-permute-start.46 = (bf16[96,768]{1,0:T(8,128)(2,1)}, bf16[96,768]{1,0:T(8,128)(2,1)}, u32[]{:S(2)}, u32[]{:S(2)}) collective-permute-start(bf16[96,768]{1,0:T(8,128)(2,1)} %bitcast.53), channel_id=1, source_target_pairs={{0,16},{4,20},{8,24},{12,28},{16,0},{20,4},{24,8},{28,12},{1,17},{... | collective-permute-start | bytes 442376 | tf_op jit(solution)/shard_map/ppermute | solution.py:176
  209.3 13.4 %collective-permute-start.38 = (bf16[256,768]{1,0:T(8,128)(2,1)S(1)}, bf16[256,768]{1,0:T(8,128)(2,1)S(1)}, u32[]{:S(2)}, u32[]{:S(2)}) collective-permute-start(bf16[256,768]{1,0:T(8,128)(2,1)S(1)} %bitcast.124), channel_id=1, source_target_pairs={{0,8},{4,12},{8,0},{12,4},{16,24},{20,28},{24,16},{28,20},{1,9},{5... | collective-permute-start | bytes 1179656 | tf_op jit(solution)/shard_map/ppermute | solution.py:176
  215.2 18.1 %collective-permute-start.60 = (bf16[256,768]{1,0:T(8,128)(2,1)S(1)}, bf16[256,768]{1,0:T(8,128)(2,1)S(1)}, u32[]{:S(2)}, u32[]{:S(2)}) collective-permute-start(bf16[256,768]{1,0:T(8,128)(2,1)S(1)} %fusion.45), channel_id=1, source_target_pairs={{0,8},{4,12},{8,0},{12,4},{16,24},{20,28},{24,16},{28,20},{1,9},{5... | collective-permute-start | bytes 1179656 | tf_op jit(solution)/shard_map/ppermute | solution.py:176
  220.3 13.1 %collective-permute-start.49 = (bf16[96,768]{1,0:T(8,128)(2,1)S(1)}, bf16[96,768]{1,0:T(8,128)(2,1)S(1)}, u32[]{:S(2)}, u32[]{:S(2)}) collective-permute-start(bf16[96,768]{1,0:T(8,128)(2,1)S(1)} %bitcast.138), channel_id=1, source_target_pairs={{0,28},{4,24},{8,20},{12,16},{16,12},{20,8},{24,4},{28,0},{1,29},{... | collective-permute-start | bytes 442376 | tf_op jit(solution)/shard_map/ppermute | solution.py:176
  239.9 93.1 %collective-permute-start.107 = (bf16[384,768]{1,0:T(8,128)(2,1)}, bf16[384,768]{1,0:T(8,128)(2,1)}, u32[]{:S(2)}, u32[]{:S(2)}) collective-permute-start(bf16[384,768]{1,0:T(8,128)(2,1)} %dynamic-slice_convert_fusion), channel_id=1, source_target_pairs={{0,16},{4,20},{8,24},{12,28},{16,0},{20,4},{24,8},{28,12},{1,17},{... | collective-permute-start | bytes 1769480 | tf_op jit(solution)/shard_map/ppermute | solution.py:176
  256.3 13.3 %collective-permute-start.101 = (bf16[96,768]{1,0:T(8,128)(2,1)}, bf16[96,768]{1,0:T(8,128)(2,1)}, u32[]{:S(2)}, u32[]{:S(2)}) collective-permute-start(bf16[96,768]{1,0:T(8,128)(2,1)} %get-tuple-element.134), channel_id=1, source_target_pairs={{0,24},{4,28},{8,16},{12,20},{16,8},{20,12},{24,0},{28,4},{1,25},{... | collective-permute-start | bytes 442376 | tf_op jit(solution)/shard_map/ppermute | solution.py:176
  260.2 13.1 %collective-permute-start.98 = (bf16[96,768]{1,0:T(8,128)(2,1)}, bf16[96,768]{1,0:T(8,128)(2,1)}, u32[]{:S(2)}, u32[]{:S(2)}) collective-permute-start(bf16[96,768]{1,0:T(8,128)(2,1)} %get-tuple-element.137), channel_id=1, source_target_pairs={{0,4},{4,0},{8,12},{12,8},{16,20},{20,16},{24,28},{28,24},{1,5},{5... | collective-permute-start | bytes 442376 | tf_op jit(solution)/shard_map/ppermute | solution.py:176
  269.6 68.3 %collective-permute-start.55 = (bf16[256,768]{1,0:T(8,128)(2,1)}, bf16[256,768]{1,0:T(8,128)(2,1)}, u32[]{:S(2)}, u32[]{:S(2)}) collective-permute-start(bf16[256,768]{1,0:T(8,128)(2,1)} %get-tuple-element.149), channel_id=1, source_target_pairs={{0,4},{4,0},{8,12},{12,8},{16,20},{20,16},{24,28},{28,24},{1,5},{5... | collective-permute-start | bytes 1179656 | tf_op jit(solution)/shard_map/ppermute | solution.py:176
  316.8 13.5 %collective-permute-start.105 = (bf16[24,3072]{1,0:T(8,128)(2,1)S(1)}, bf16[24,3072]{1,0:T(8,128)(2,1)S(1)}, u32[]{:S(2)}, u32[]{:S(2)}) collective-permute-start(bf16[24,3072]{1,0:T(8,128)(2,1)S(1)} %get-tuple-element.155), channel_id=1, source_target_pairs={{0,2},{1,3},{2,0},{3,1},{4,6},{5,7},{6,4},{7,5},{8,10},{9,11},{10,... | collective-permute-start | bytes 442376 | tf_op jit(solution)/shard_map/ppermute | solution.py:176
  316.8 13.5 %collective-permute-start.106 = (bf16[24,3072]{1,0:T(8,128)(2,1)S(1)}, bf16[24,3072]{1,0:T(8,128)(2,1)S(1)}, u32[]{:S(2)}, u32[]{:S(2)}) collective-permute-start(bf16[24,3072]{1,0:T(8,128)(2,1)S(1)} %get-tuple-element.154), channel_id=1, source_target_pairs={{0,3},{1,2},{2,1},{3,0},{4,7},{5,6},{6,5},{7,4},{8,11},{9,10},{10,... | collective-permute-start | bytes 442376 | tf_op jit(solution)/shard_map/ppermute | solution.py:176
  330.3 22.4 %collective-permute-start.62 = (bf16[256,768]{1,0:T(8,128)(2,1)S(1)}, bf16[256,768]{1,0:T(8,128)(2,1)S(1)}, u32[]{:S(2)}, u32[]{:S(2)}) collective-permute-start(bf16[256,768]{1,0:T(8,128)(2,1)S(1)} %get-tuple-element.146), channel_id=1, source_target_pairs={{0,4},{4,0},{8,12},{12,8},{16,20},{20,16},{24,28},{28,24},{1,5},{5... | collective-permute-start | bytes 1179656 | tf_op jit(solution)/shard_map/ppermute | solution.py:176
  332.2 20.5 %collective-permute-start.64 = (bf16[256,768]{1,0:T(8,128)(2,1)S(1)}, bf16[256,768]{1,0:T(8,128)(2,1)S(1)}, u32[]{:S(2)}, u32[]{:S(2)}) collective-permute-start(bf16[256,768]{1,0:T(8,128)(2,1)S(1)} %add_convert_fusion.3), channel_id=1, source_target_pairs={{0,8},{4,12},{8,0},{12,4},{16,24},{20,28},{24,16},{28,20},{1,9},{5... | collective-permute-start | bytes 1179656 | tf_op jit(solution)/shard_map/ppermute | solution.py:176
  337.9 13.1 %collective-permute-start.109 = (bf16[96,768]{1,0:T(8,128)(2,1)S(1)}, bf16[96,768]{1,0:T(8,128)(2,1)S(1)}, u32[]{:S(2)}, u32[]{:S(2)}) collective-permute-start(bf16[96,768]{1,0:T(8,128)(2,1)S(1)} %get-tuple-element.152), channel_id=1, source_target_pairs={{0,2},{1,3},{2,0},{3,1},{4,6},{5,7},{6,4},{7,5},{8,10},{9,11},{10,... | collective-permute-start | bytes 442376 | tf_op jit(solution)/shard_map/ppermute | solution.py:176
  337.9 14.0 %collective-permute-start.110 = (bf16[96,768]{1,0:T(8,128)(2,1)S(1)}, bf16[96,768]{1,0:T(8,128)(2,1)S(1)}, u32[]{:S(2)}, u32[]{:S(2)}) collective-permute-start(bf16[96,768]{1,0:T(8,128)(2,1)S(1)} %get-tuple-element.151), channel_id=1, source_target_pairs={{0,3},{1,2},{2,1},{3,0},{4,7},{5,6},{6,5},{7,4},{8,11},{9,10},{10,... | collective-permute-start | bytes 442376 | tf_op jit(solution)/shard_map/ppermute | solution.py:176
  425.6 39.8 %collective-permute-start.88 = (bf16[96,768]{1,0:T(8,128)(2,1)}, bf16[96,768]{1,0:T(8,128)(2,1)}, u32[]{:S(2)}, u32[]{:S(2)}) collective-permute-start(bf16[96,768]{1,0:T(8,128)(2,1)} %get-tuple-element.142), channel_id=1, source_target_pairs={{0,4},{4,0},{8,12},{12,8},{16,20},{20,16},{24,28},{28,24},{1,5},{5... | collective-permute-start | bytes 442376 | tf_op jit(solution)/shard_map/ppermute | solution.py:176
  425.6 39.8 %collective-permute-start.90 = (bf16[96,768]{1,0:T(8,128)(2,1)}, bf16[96,768]{1,0:T(8,128)(2,1)}, u32[]{:S(2)}, u32[]{:S(2)}) collective-permute-start(bf16[96,768]{1,0:T(8,128)(2,1)} %get-tuple-element.141), channel_id=1, source_target_pairs={{0,4},{4,0},{8,12},{12,8},{16,20},{20,16},{24,28},{28,24},{1,5},{5... | collective-permute-start | bytes 442376 | tf_op jit(solution)/shard_map/ppermute | solution.py:176
  426.1 39.3 %collective-permute-start.92 = (bf16[96,768]{1,0:T(8,128)(2,1)}, bf16[96,768]{1,0:T(8,128)(2,1)}, u32[]{:S(2)}, u32[]{:S(2)}) collective-permute-start(bf16[96,768]{1,0:T(8,128)(2,1)} %get-tuple-element.140), channel_id=1, source_target_pairs={{0,4},{4,0},{8,12},{12,8},{16,20},{20,16},{24,28},{28,24},{1,5},{5... | collective-permute-start | bytes 442376 | tf_op jit(solution)/shard_map/ppermute | solution.py:176
  426.1 46.8 %collective-permute-start.87 = (bf16[96,768]{1,0:T(8,128)(2,1)}, bf16[96,768]{1,0:T(8,128)(2,1)}, u32[]{:S(2)}, u32[]{:S(2)}) collective-permute-start(bf16[96,768]{1,0:T(8,128)(2,1)} %get-tuple-element.139), channel_id=1, source_target_pairs={{0,4},{4,0},{8,12},{12,8},{16,20},{20,16},{24,28},{28,24},{1,5},{5... | collective-permute-start | bytes 442376 | tf_op jit(solution)/shard_map/ppermute | solution.py:176
  465.3 23.7 %collective-permute-start.78 = (bf16[96,2304]{1,0:T(8,128)(2,1)}, bf16[96,2304]{1,0:T(8,128)(2,1)}, u32[]{:S(2)}, u32[]{:S(2)}) collective-permute-start(bf16[96,2304]{1,0:T(8,128)(2,1)} %get-tuple-element.109), channel_id=1, source_target_pairs={{0,4},{4,0},{8,12},{12,8},{16,20},{20,16},{24,28},{28,24},{1,5},{5... | collective-permute-start | bytes 1327112 | tf_op jit(solution)/shard_map/ppermute | solution.py:176
  472.9 16.6 %collective-permute-start.80 = (bf16[96,2304]{1,0:T(8,128)(2,1)}, bf16[96,2304]{1,0:T(8,128)(2,1)S(1)}, u32[]{:S(2)}, u32[]{:S(2)}) collective-permute-start(bf16[96,2304]{1,0:T(8,128)(2,1)} %get-tuple-element.108), channel_id=1, source_target_pairs={{0,4},{4,0},{8,12},{12,8},{16,20},{20,16},{24,28},{28,24},{1,5},{5... | collective-permute-start | bytes 1327112 | tf_op jit(solution)/shard_map/ppermute | solution.py:176
  474.4 15.2 %collective-permute-start.82 = (bf16[96,2304]{1,0:T(8,128)(2,1)}, bf16[96,2304]{1,0:T(8,128)(2,1)S(1)}, u32[]{:S(2)}, u32[]{:S(2)}) collective-permute-start(bf16[96,2304]{1,0:T(8,128)(2,1)} %get-tuple-element.107), channel_id=1, source_target_pairs={{0,4},{4,0},{8,12},{12,8},{16,20},{20,16},{24,28},{28,24},{1,5},{5... | collective-permute-start | bytes 1327112 | tf_op jit(solution)/shard_map/ppermute | solution.py:176
  477.6 19.2 %collective-permute-start.66 = (bf16[2,128,768]{2,1,0:T(8,128)(2,1)}, bf16[2,128,768]{2,1,0:T(8,128)(2,1)S(1)}, u32[]{:S(2)}, u32[]{:S(2)}) collective-permute-start(bf16[2,128,768]{2,1,0:T(8,128)(2,1)} %get-tuple-element.114), channel_id=1, source_target_pairs={{0,4},{4,0},{8,12},{12,8},{16,20},{20,16},{24,28},{28,24},{1,5},{5... | collective-permute-start | bytes 1179656 | tf_op jit(solution)/shard_map/ppermute | solution.py:176
  496.8 21.8 %collective-permute-start.81 = (bf16[96,2304]{1,0:T(8,128)(2,1)S(1)}, bf16[96,2304]{1,0:T(8,128)(2,1)S(1)}, u32[]{:S(2)}, u32[]{:S(2)}) collective-permute-start(bf16[96,2304]{1,0:T(8,128)(2,1)S(1)} %get-tuple-element.112), channel_id=1, source_target_pairs={{0,16},{4,20},{8,24},{12,28},{16,0},{20,4},{24,8},{28,12},{1,17},{... | collective-permute-start | bytes 1327112 | tf_op jit(solution)/shard_map/ppermute | solution.py:176
  497.8 21.7 %collective-permute-start.83 = (bf16[96,2304]{1,0:T(8,128)(2,1)S(1)}, bf16[96,2304]{1,0:T(8,128)(2,1)S(1)}, u32[]{:S(2)}, u32[]{:S(2)}) collective-permute-start(bf16[96,2304]{1,0:T(8,128)(2,1)S(1)} %get-tuple-element.111), channel_id=1, source_target_pairs={{0,24},{4,28},{8,16},{12,20},{16,8},{20,12},{24,0},{28,4},{1,25},{... | collective-permute-start | bytes 1327112 | tf_op jit(solution)/shard_map/ppermute | solution.py:176
  499.7 22.8 %collective-permute-start.65 = (bf16[2,128,768]{2,1,0:T(8,128)(2,1)S(1)}, bf16[2,128,768]{2,1,0:T(8,128)(2,1)S(1)}, u32[]{:S(2)}, u32[]{:S(2)}) collective-permute-start(bf16[2,128,768]{2,1,0:T(8,128)(2,1)S(1)} %copy-done.31), channel_id=1, source_target_pairs={{0,4},{4,0},{8,12},{12,8},{16,20},{20,16},{24,28},{28,24},{1,5},{5... | collective-permute-start | bytes 1179656 | tf_op jit(solution)/shard_map/ppermute | solution.py:176
  500.1 26.4 %collective-permute-start.67 = (bf16[2,128,768]{2,1,0:T(8,128)(2,1)S(1)}, bf16[2,128,768]{2,1,0:T(8,128)(2,1)S(1)}, u32[]{:S(2)}, u32[]{:S(2)}) collective-permute-start(bf16[2,128,768]{2,1,0:T(8,128)(2,1)S(1)} %get-tuple-element.117), channel_id=1, source_target_pairs={{0,8},{4,12},{8,0},{12,4},{16,24},{20,28},{24,16},{28,20},{1,9},{5... | collective-permute-start | bytes 1179656 | tf_op jit(solution)/shard_map/ppermute | solution.py:176
  508.5 26.9 %collective-permute-start.69 = (bf16[2,128,768]{2,1,0:T(8,128)(2,1)S(1)}, bf16[2,128,768]{2,1,0:T(8,128)(2,1)S(1)}, u32[]{:S(2)}, u32[]{:S(2)}) collective-permute-start(bf16[2,128,768]{2,1,0:T(8,128)(2,1)S(1)} %get-tuple-element.118), channel_id=1, source_target_pairs={{0,16},{4,20},{8,24},{12,28},{16,0},{20,4},{24,8},{28,12},{1,17},{... | collective-permute-start | bytes 1179656 | tf_op jit(solution)/shard_map/ppermute | solution.py:176
  518.6 16.8 %collective-permute-start.71 = (bf16[2,128,768]{2,1,0:T(8,128)(2,1)S(1)}, bf16[2,128,768]{2,1,0:T(8,128)(2,1)S(1)}, u32[]{:S(2)}, u32[]{:S(2)}) collective-permute-start(bf16[2,128,768]{2,1,0:T(8,128)(2,1)S(1)} %get-tuple-element.119), channel_id=1, source_target_pairs={{0,24},{4,28},{8,16},{12,20},{16,8},{20,12},{24,0},{28,4},{1,25},{... | collective-permute-start | bytes 1179656 | tf_op jit(solution)/shard_map/ppermute | solution.py:176
  521.0 15.4 %collective-permute-start.84 = (bf16[24,2304]{1,0:T(8,128)(2,1)S(1)}, bf16[24,2304]{1,0:T(8,128)(2,1)S(1)}, u32[]{:S(2)}, u32[]{:S(2)}) collective-permute-start(bf16[24,2304]{1,0:T(8,128)(2,1)S(1)} %get-tuple-element.156), channel_id=1, source_target_pairs={{0,1},{1,0},{2,3},{3,2},{4,5},{5,4},{6,7},{7,6},{8,9},{9,8},{10,11... | collective-permute-start | bytes 331784 | tf_op jit(solution)/shard_map/ppermute | solution.py:176
  522.5 13.9 %collective-permute-start.85 = (bf16[24,2304]{1,0:T(8,128)(2,1)S(1)}, bf16[24,2304]{1,0:T(8,128)(2,1)S(1)}, u32[]{:S(2)}, u32[]{:S(2)}) collective-permute-start(bf16[24,2304]{1,0:T(8,128)(2,1)S(1)} %get-tuple-element.158), channel_id=1, source_target_pairs={{0,2},{1,3},{2,0},{3,1},{4,6},{5,7},{6,4},{7,5},{8,10},{9,11},{10,... | collective-permute-start | bytes 331784 | tf_op jit(solution)/shard_map/ppermute | solution.py:176
  (127 other events, 1149.1 us)
